TPU v7x, 512 devices: a whole 4x8x8 slice. The times are simulated.
512 devices in a mesh: wave: 32 (over y, x), lev: 16 (over z, core).
Axes of the slice: x: 4, y: 8, z: 8, core: 2. Of those that a mesh axis runs over, the one named last changes fastest.
Arguments:
- spec: bfloat16 [2, 3, 16, 1280, 1280], P(None, None, 'lev', 'wave'), may hold values from -0.0048828125 to 0.0048828125
- legendre: bfloat16 [1280, 1280, 64], P('wave', 'lev'), may hold values from -4 to 4
- mids: int32 [1280], replicated, may hold values from 0 to 1279, each once
- band_lats: int32 [32], replicated, may hold values from 1 to 8, 128 in all
- nlon: int32 [64], replicated, may hold values from 1296 to 5136, as said below
Outputs:
- grid: bfloat16 [256, 3, 16, 5136], P('wave', None, 'lev')
Inputs may be any that keep to these rules, and one draw needn't show every extreme that they name: `mids`: each wavenumber appears in exactly one slot; index i of wave holds slots i * 40 to (i + 1) * 40 - 1. `band_lats`: the bands sum to 128 latitudes. `nlon`: every entry is 4 i + 16 for a whole number i.
All inputs are finite; a program needn't handle non-finite values.
Results may differ from a plain program's by a relative error of at most 0.02.
Values may be sent and summed in bfloat16 or wider, within the bound.
A program may use at most 128 MiB of HBM per device.

v0:
```python
import jax
import jax.numpy as jnp
from jax import lax
from jax.experimental import pallas as pl
from jax.experimental.pallas import tpu as pltpu
from jax.sharding import PartitionSpec as P

LAT_MAX = 8
NLON_MAX = 5136
KH = 41
WAVES = 32
LEVS = 16
CHIPS = 8
SLOTS = 40
GROUP = 5
MW = 1280
HALF = 640
BLOCK = 80
PAIRS = 64
LATS = 128
TWO_PI = 6.283185307179586
F32 = jnp.float32
BF16 = jnp.bfloat16
MESH = pl.DeviceIdType.MESH

SIN = []
_term = TWO_PI
for _i in range(6):
    SIN.append(_term)
    _term = -_term * TWO_PI * TWO_PI / ((2 * _i + 2) * (2 * _i + 3))


def quarter_sine(y):
    y2 = y * y
    acc = jnp.full_like(y2, SIN[-1])
    for c in SIN[-2::-1]:
        acc = acc * y2 + c
    return acc * y


def cos_sin(steps, cycle, inverse):
    rest = steps - jnp.floor(steps * inverse + 0.5) * cycle
    t = rest * inverse
    a = jnp.abs(t)
    folded = jnp.where(a > 0.25, jnp.where(t < 0, -0.5, 0.5) - t, t)
    return quarter_sine(0.25 - a), quarter_sine(folded)


def nt_dot(a, b):
    return lax.dot_general(a, b, (((1,), (1,)), ((), ())), preferred_element_type=F32)


def kernel(
    mids_ref, bands_ref, nlon_ref, spec_ref, leg_ref, mrow_ref, out_ref,
    spec_f, send_s, send_l, recv_s, recv_l, rhs, sums, send_r, recv_x,
    onehot, send_y, recv_z, zf, zs, expand, mcol, cosc, sinc, tw, mod, lat,
    ss_send, ss_recv, sl_send, sl_recv, sx_send, sx_recv, sz_send, sz_recv,
):
    w = lax.axis_index("wave")
    me = lax.axis_index("lev")
    z = me // 2
    c = me - 2 * z
    half = z // 4

    barrier = pltpu.get_barrier_semaphore()

    def greet_lev(k, carry):
        pl.semaphore_signal(barrier, inc=1, device_id={"lev": lax.rem(me + k, LEVS)}, device_id_type=MESH)
        return carry

    def greet_wave(k, carry):
        pl.semaphore_signal(barrier, inc=1, device_id={"wave": lax.rem(w + k, WAVES)}, device_id_type=MESH)
        return carry

    lax.fori_loop(1, LEVS, greet_lev, 0)
    lax.fori_loop(1, WAVES, greet_wave, 0)

    for tile in range(10):
        spec_f[tile, 0:240, :] = spec_ref[:, 128 * tile:128 * tile + 128].astype(F32)
        spec_f[tile, 240:256, :] = jnp.zeros((16, 128), F32)

    unit = jnp.where(
        lax.broadcasted_iota(jnp.int32, (BLOCK, BLOCK), 0) == lax.broadcasted_iota(jnp.int32, (BLOCK, BLOCK), 1),
        1.0, 0.0,
    ).astype(BF16)

    pl.semaphore_wait(barrier, LEVS + WAVES - 2)

    def spec_copy(k, h):
        to = lax.rem(z + k, CHIPS)
        return pltpu.make_async_remote_copy(
            src_ref=send_s.at[to, h], dst_ref=recv_s.at[me], send_sem=ss_send.at[2 * k + h],
            recv_sem=ss_recv.at[me], device_id={"lev": 2 * to + h}, device_id_type=MESH,
        )

    def leg_copy(k):
        to = lax.rem(z + k, CHIPS)
        return pltpu.make_async_remote_copy(
            src_ref=send_l.at[to], dst_ref=recv_l.at[lax.rem(me, 8)], send_sem=sl_send.at[k],
            recv_sem=sl_recv.at[lax.rem(me, 8)], device_id={"lev": 2 * to + half}, device_id_type=MESH,
        )

    def prepare(k):
        to = lax.rem(z + k, CHIPS)
        for tile in range(10):
            rows = spec_f[tile, pl.ds(to, 32, stride=8), :].astype(BF16)
            send_s[to, tile // 5, :, 128 * (tile % 5):128 * (tile % 5) + 128] = rows
        for p in range(3):
            first = leg_ref[16 * p + to]
            second = leg_ref[16 * p + 8 + to] if p < 2 else jnp.zeros((PAIRS, BLOCK), BF16)
            stacked = jnp.concatenate([first, second], axis=0)
            send_l[to, BLOCK * p:BLOCK * p + BLOCK, :] = nt_dot(unit, stacked).astype(BF16)

    def send_far(i, carry):
        k = CHIPS - i
        prepare(k)
        for h in range(2):
            spec_copy(k, h).start()
        leg_copy(k).start()
        return carry

    lax.fori_loop(1, CHIPS, send_far, 0)
    prepare(0)
    for h in range(2):
        @pl.when(c == h)
        def _():
            pltpu.make_async_copy(send_s.at[z, h], recv_s.at[me], ss_recv.at[me]).start()

        @pl.when(c != h)
        def _():
            spec_copy(0, h).start()

    @pl.when(c == half)
    def _():
        pltpu.make_async_copy(send_l.at[z], recv_l.at[lax.rem(me, 8)], sl_recv.at[lax.rem(me, 8)]).start()

    @pl.when(c != half)
    def _():
        leg_copy(0).start()

    start = jnp.int32(0)
    own_start = jnp.int32(0)
    sub16 = lax.broadcasted_iota(jnp.int32, (16, 256), 0)
    lane = lax.broadcasted_iota(jnp.int32, (16, 256), 1)
    lat_of = jnp.where(lane < 128, lane & 63, 127 - (lane & 63))
    for e in range(WAVES // 2):
        count_a, count_b = bands_ref[2 * e], bands_ref[2 * e + 1]
        start_b = start + count_a
        own_start = jnp.where(w == 2 * e, start, jnp.where(w == 2 * e + 1, start_b, own_start))
        inner = sub16 & 7
        wanted = jnp.where(sub16 < 8, start, start_b) + inner
        filled = inner < jnp.where(sub16 < 8, count_a, count_b)
        match = jnp.where(filled, wanted, -1) == lat_of
        onehot[16 * e:16 * e + 16, :] = jnp.where(match, 1.0, 0.0).astype(BF16)
        start = start_b + count_b

    def cycle_of(slot):
        latitude = jnp.minimum(own_start + slot, LATS - 1)
        pair = jnp.where(latitude < PAIRS, latitude, LATS - 1 - latitude)
        return nlon_ref[pair]

    krow = lax.broadcasted_iota(jnp.int32, (128, 256), 0)
    klane = lax.broadcasted_iota(jnp.int32, (128, 256), 1)
    col = klane & 127
    channel = jnp.where(col >= KH, 1, 0) + jnp.where(col >= 2 * KH, 1, 0) + jnp.where(col >= 3 * KH, 100, 0)
    base = krow - (GROUP * channel + jnp.where(klane >= 128, 15, 0))

    def fill_expand(i, carry):
        zl = i // GROUP
        match = base == zl * 32 + (i - GROUP * zl)
        expand[i] = jnp.where(match, 1.0, 0.0).astype(BF16)
        return carry

    lax.fori_loop(0, 20, fill_expand, 0)

    for t in range(10):
        row = jnp.broadcast_to(mrow_ref[0:1, 128 * t:128 * t + 128], (128, 128))
        mcol[128 * t:128 * t + 128, :] = row.T

    col1 = lax.broadcasted_iota(jnp.int32, (1, 128), 1)
    channel1 = jnp.where(col1 >= KH, 1, 0) + jnp.where(col1 >= 2 * KH, 1, 0)
    coarse_steps = (128 * (col1 - KH * channel1)).astype(F32)
    a_steps = (16 * lax.broadcasted_iota(jnp.int32, (8, 128), 0)).astype(F32)
    b_steps = lax.broadcasted_iota(jnp.int32, (16, 128), 0).astype(F32)

    def tables(slot, carry):
        cycle = jnp.full((1, 128), cycle_of(slot), jnp.int32).astype(F32)
        inverse = 1.0 / cycle

        def coarse(i, inner_carry):
            at = pl.multiple_of(128 * i, 128)
            cos_part, sin_part = cos_sin(mcol[pl.ds(at, 128), :] * coarse_steps, cycle, inverse)
            cosc[slot, pl.ds(at, 128), :] = cos_part
            sinc[slot, pl.ds(at, 128), :] = sin_part
            return inner_carry

        lax.fori_loop(0, 10, coarse, 0)

        def fine(i, inner_carry):
            at = pl.multiple_of(128 * i, 128)
            m = mrow_ref[0:1, pl.ds(at, 128)]
            weight = jnp.where(m == 0, 1.0, 2.0)
            weight = jnp.where(2 * m < cycle, weight, 0.0)
            cos_a, sin_a = cos_sin(m * a_steps, cycle, inverse)
            cos_b, sin_b = cos_sin(m * b_steps, cycle, inverse)
            cos_a = cos_a * weight
            sin_a = sin_a * weight
            for a in range(8):
                ca, sa = cos_a[a:a + 1, :], sin_a[a:a + 1, :]
                tw[slot, 16 * a:16 * a + 16, pl.ds(at, 128)] = (ca * cos_b - sa * sin_b).astype(BF16)
                other = pl.multiple_of(at + MW, 128)
                tw[slot, 16 * a:16 * a + 16, pl.ds(other, 128)] = (-(sa * cos_b + ca * sin_b)).astype(BF16)
            return inner_carry

        lax.fori_loop(0, 10, fine, 0)
        return carry

    lax.fori_loop(0, LAT_MAX, tables, 0)

    def wait_spec(k, carry):
        pltpu.make_async_copy(recv_s.at[k], recv_s.at[k], ss_recv.at[k]).wait()
        return carry

    def wait_leg(k, carry):
        pltpu.make_async_copy(recv_l.at[k], recv_l.at[k], sl_recv.at[k]).wait()
        return carry

    lax.fori_loop(0, LEVS, wait_spec, 0)
    lax.fori_loop(0, 8, wait_leg, 0)

    left = recv_s[...].reshape(512, HALF)
    row_r = lax.broadcasted_iota(jnp.int32, (512, 256), 0) & 31
    j_r = row_r - GROUP * jnp.floor((row_r.astype(F32) + 0.5) * 0.2).astype(jnp.int32)
    lane_r = lax.broadcasted_iota(jnp.int32, (512, 256), 1)
    degree = lax.broadcasted_iota(jnp.int32, (HALF, 128), 0) + HALF * c
    lane_n = lax.broadcasted_iota(jnp.int32, (HALF, 128), 1)
    for p in range(3):
        m_a = mids_ref[SLOTS * w + 16 * p + z]
        m_b = mids_ref[SLOTS * w + 16 * p + 8 + z] if p < 2 else m_a
        m = jnp.where(lane_n < PAIRS, m_a, m_b)
        table = recv_l[:, BLOCK * p:BLOCK * p + BLOCK, :].reshape(HALF, 128).astype(F32)
        table = jnp.where(degree >= m, table, 0.0)
        rhs[:, 0:128] = table.astype(BF16)
        rhs[:, 128:256] = jnp.where(((degree + m) & 1) == 1, -table, table).astype(BF16)
        terms = jnp.dot(left, rhs[...], preferred_element_type=F32)
        if p == 0:
            sums[...] = terms
        else:
            sums[...] = jnp.where(j_r >= 2 * p, terms, sums[...])
    keep = ((lane_r & 127) < PAIRS) == ((j_r & 1) == 0)
    send_r[...] = jnp.where(keep, sums[...], 0.0).astype(BF16).reshape(LEVS, 32, 256)

    def level_copy(k):
        to = lax.rem(me + k, LEVS)
        return pltpu.make_async_remote_copy(
            src_ref=send_r.at[to], dst_ref=recv_x.at[me], send_sem=sx_send.at[k],
            recv_sem=sx_recv.at[me], device_id={"lev": to}, device_id_type=MESH,
        )

    def send_level(k, carry):
        level_copy(k).start()
        return carry

    lax.fori_loop(1, LEVS, send_level, 0)
    pltpu.make_async_copy(send_r.at[me], recv_x.at[me], sx_recv.at[me]).start()

    def wait_level(k, carry):
        pltpu.make_async_copy(recv_x.at[k], recv_x.at[k], sx_recv.at[k]).wait()
        return carry

    lax.fori_loop(0, LEVS, wait_level, 0)

    got = recv_x[...].astype(F32).reshape(CHIPS, 2, 32, 256)
    level_sums = (got[:, 0] + got[:, 1]).reshape(256, 256).astype(BF16)
    by_slot = nt_dot(onehot[...], level_sums)
    low = by_slot[:, 0:128].reshape(WAVES, 8, 128)
    high = by_slot[:, 128:256].reshape(WAVES, 8, 128)
    send_y[...] = jnp.concatenate([low, high], axis=1).astype(BF16)

    def band_copy(k):
        to = lax.rem(w + k, WAVES)
        return pltpu.make_async_remote_copy(
            src_ref=send_y.at[to], dst_ref=recv_z.at[w], send_sem=sz_send.at[k],
            recv_sem=sz_recv.at[w], device_id={"wave": to}, device_id_type=MESH,
        )

    def send_band(k, carry):
        band_copy(k).start()
        return carry

    lax.fori_loop(1, WAVES, send_band, 0)
    pltpu.make_async_copy(send_y.at[w], recv_z.at[w], sz_recv.at[w]).start()

    def wait_band(k, carry):
        pltpu.make_async_copy(recv_z.at[k], recv_z.at[k], sz_recv.at[k]).wait()
        return carry

    lax.fori_loop(0, WAVES, wait_band, 0)

    zf[...] = recv_z[...].astype(F32).reshape(512, 128)
    for slot in range(LAT_MAX):
        zs[64 * slot:64 * slot + 64, :] = zf[pl.ds(slot, 64, stride=8), :].astype(BF16)

    def modulate(i, carry):
        both = jnp.dot(zs[...], expand[i], preferred_element_type=F32)
        at = pl.multiple_of(64 * i, 64)
        other = pl.multiple_of(64 * i + MW, 64)
        for slot in range(LAT_MAX):
            re = both[64 * slot:64 * slot + 64, 0:128]
            im = both[64 * slot:64 * slot + 64, 128:256]
            cos_part = cosc[slot, pl.ds(at, 64), :]
            sin_part = sinc[slot, pl.ds(at, 64), :]
            mod[slot, pl.ds(at, 64), :] = (re * cos_part - im * sin_part).astype(BF16)
            mod[slot, pl.ds(other, 64), :] = (re * sin_part + im * cos_part).astype(BF16)
        return carry

    lax.fori_loop(0, 20, modulate, 0)

    def transform(slot, carry):
        points = jnp.dot(tw[slot], mod[slot], preferred_element_type=F32)
        lat[pl.ds(slot, 128, stride=8), :] = points.T
        return carry

    lax.fori_loop(0, LAT_MAX, transform, 0)

    slot_of = lax.broadcasted_iota(jnp.int32, (8, 128), 0)
    lon = lax.broadcasted_iota(jnp.int32, (8, 128), 1)
    cycles = jnp.zeros((8, 128), jnp.int32)
    for slot in range(LAT_MAX):
        cycles = jnp.where(slot_of == slot, cycle_of(slot), cycles)
    for f in range(3):
        for kh in range(KH):
            at = 8 * (KH * f + kh)
            width = min(128, NLON_MAX - 128 * kh)
            tile = jnp.where(lon + 128 * kh < cycles, lat[at:at + 8, :], 0.0).astype(BF16)
            out_ref[f, :, 128 * kh:128 * kh + width] = tile[:, 0:width]

    def sent_far(k, carry):
        for h in range(2):
            spec_copy(k, h).wait_send()
        leg_copy(k).wait_send()
        return carry

    lax.fori_loop(1, CHIPS, sent_far, 0)
    for h in range(2):
        @pl.when(c != h)
        def _():
            spec_copy(0, h).wait_send()

    @pl.when(c != half)
    def _():
        leg_copy(0).wait_send()

    def sent_level(k, carry):
        level_copy(k).wait_send()
        return carry

    lax.fori_loop(1, LEVS, sent_level, 0)

    def sent_band(k, carry):
        band_copy(k).wait_send()
        return carry

    lax.fori_loop(1, WAVES, sent_band, 0)


def on_device(spec, legendre, mids, band_lats, nlon):
    spec_rows = spec.reshape(240, MW)
    tables = jnp.transpose(legendre, (0, 2, 1))
    order = jnp.transpose(mids.reshape(WAVES, GROUP, 2, 4), (3, 1, 0, 2)).reshape(1, MW).astype(F32)
    smem = pl.BlockSpec(memory_space=pltpu.SMEM)
    vmem = pl.BlockSpec(memory_space=pltpu.VMEM)
    dma = pltpu.SemaphoreType.DMA
    planes = pl.pallas_call(
        kernel,
        out_shape=jax.ShapeDtypeStruct((3, LAT_MAX, NLON_MAX), BF16),
        in_specs=[smem, smem, smem, vmem, vmem, vmem],
        out_specs=vmem,
        scratch_shapes=[
            pltpu.VMEM((10, 256, 128), F32),
            pltpu.VMEM((CHIPS, 2, 32, HALF), BF16),
            pltpu.VMEM((CHIPS, 3 * BLOCK, 128), BF16),
            pltpu.VMEM((LEVS, 32, HALF), BF16),
            pltpu.VMEM((8, 3 * BLOCK, 128), BF16),
            pltpu.VMEM((HALF, 256), BF16),
            pltpu.VMEM((512, 256), F32),
            pltpu.VMEM((LEVS, 32, 256), BF16),
            pltpu.VMEM((LEVS, 32, 256), BF16),
            pltpu.VMEM((256, 256), BF16),
            pltpu.VMEM((WAVES, 16, 128), BF16),
            pltpu.VMEM((WAVES, 16, 128), BF16),
            pltpu.VMEM((512, 128), F32),
            pltpu.VMEM((512, 128), BF16),
            pltpu.VMEM((20, 128, 256), BF16),
            pltpu.VMEM((MW, 128), F32),
            pltpu.VMEM((LAT_MAX, MW, 128), F32),
            pltpu.VMEM((LAT_MAX, MW, 128), F32),
            pltpu.VMEM((LAT_MAX, 128, 2 * MW), BF16),
            pltpu.VMEM((LAT_MAX, 2 * MW, 128), BF16),
            pltpu.VMEM((1024, 128), F32),
            dma((2 * CHIPS,)), dma((LEVS,)), dma((CHIPS,)), dma((8,)),
            dma((LEVS,)), dma((LEVS,)), dma((WAVES,)), dma((WAVES,)),
        ],
        compiler_params=pltpu.CompilerParams(
            collective_id=0, has_side_effects=True, vmem_limit_bytes=52 * 2**20
        ),
    )(mids, band_lats, nlon, spec_rows, tables, order)
    return jnp.transpose(planes, (1, 0, 2)).reshape(LAT_MAX, 3, 1, NLON_MAX)


def solution(mesh):
    in_specs = (P(None, None, "lev", "wave", None), P("wave", "lev", None), P(), P(), P())
    out_specs = P("wave", None, "lev", None)
    return jax.shard_map(
        on_device, mesh=mesh, in_specs=in_specs, out_specs=out_specs, check_vma=False
    )
```

profile of v0, /device:TPU:1, one launch (start us, length us, event | category | flops | bytes accessed | tf_op | source)
XLA Modules:
  0.0 74.4 jit_solution(12494973525832028850)
XLA Ops:
  0.0 0.0 copy-start
  0.0 0.8 %convert_element_type.9 = f32[1280]{0:T(1024)S(1)} convert(s32[1280]{0:T(1024)} %mids_ref.1) | non-fusion elementwise | flops 1280 | bytes 10240 | tf_op jit(solution)/shard_map/convert_element_type | solution.py:370
  0.8 0.3 convert_element_type.10
  1.1 1.2 %copy.7 = f32[4,5,32,2]{3,2,1,0:T(8,128)S(1)} copy(f32[4,5,32,2]{0,3,1,2:T(2,128)S(1)} %bitcast.13) | data formatting | bytes 10240 | tf_op jit(solution)/shard_map/convert_element_type | solution.py:370
  2.3 0.0 copy-start.2
  2.3 0.0 copy-start.3
  2.3 0.0 copy-start.4
  2.3 0.2 convert_element_type.12.mrow_ref
  2.5 0.0 copy-done
  2.6 0.4 copy-done.2
  3.0 0.0 copy-done.3
  3.0 0.0 copy-done.4
  3.0 0.0 copy-start.1
  3.0 1.1 %copy-done.1 = bf16[2,3,1,40,1280]{4,3,2,1,0:T(8,128)(2,1)S(1)} copy-done((bf16[2,3,1,40,1280]{4,3,2,1,0:T(8,128)(2,1)S(1)}, bf16[2,3,1,40,1280]{4,3,2,1,0:T(8,128)(2,1)}, u32[]{:S(2)}) %copy-start.1) | copy-done | bytes 614424
  4.1 69.6 %shard_map.55 = bf16[3,8,5136]{2,1,0:T(8,128)(2,1)S(1)} custom-call(s32[1280]{0:T(1024)S(1)} %copy-done.2, s32[32]{0:T(128)S(1)} %copy-done.3, s32[64]{0:T(128)S(1)} %copy-done.4, bf16[240,1280]{1,0:T(8,128)(2,1)S(1)} %bitcast.12, bf16[40,64,80]{2,1,0:T(8,128)(2,1)S(1)} %bitcast.11, f32[1,1280]{1,0:T(1,128)S(1)} %convert_element_type.12.mrow_ref), custom_call_target="tpu_custom_call" | custom-call | tf_op jit(solution)/shard_map/pallas_call | solution.py:374
  73.7 0.7 copy.10
Async XLA Ops:
  0.0 2.5 %copy-start = (bf16[40,80,64]{1,2,0:T(8,128)(2,1)S(1)}, bf16[40,80,64]{1,2,0:T(8,128)(2,1)}, u32[]{:S(2)}) copy-start(bf16[40,80,64]{1,2,0:T(8,128)(2,1)} %param.6) | copy-start | bytes 1228804
  2.3 0.7 copy-start.2
  2.3 0.7 copy-start.3
  2.3 0.7 copy-start.4
  3.0 1.1 %copy-start.1 = (bf16[2,3,1,40,1280]{4,3,2,1,0:T(8,128)(2,1)S(1)}, bf16[2,3,1,40,1280]{4,3,2,1,0:T(8,128)(2,1)}, u32[]{:S(2)}) copy-start(bf16[2,3,1,40,1280]{4,3,2,1,0:T(8,128)(2,1)} %param.5) | copy-start | bytes 1843204
where the time goes:
time: 74.6 us; the launch traced here: 74.4 us
  Pallas kernels  69.6 us (93%)
  local copies, waits for them, and re-layouts  3.97 us (5%)
  other arithmetic  0.76 us (1%)
    pallas_call x1, Pallas kernels, on_device(): pl.pallas_call(kernel, out_shape=jax.ShapeDtypeStruct((3, LAT_MAX, NLON_M...  69.6 us
    unnamed x11, local copies, waits for them, and re-layouts  2.24 us
    convert_element_type x3, local copies, waits for them, and re-layouts, on_device(): jnp.transpose(mids.reshape(WAVES, GROUP, 2, 4), (3, 1, 0, 2)).reshape(1, MW)  1.73 us

commit v1 on v0

--- a/solution.py
+++ b/solution.py
@@ -16,6 +16,7 @@
 MW = 1280
 HALF = 640
 BLOCK = 80
+LEG_ROWS = 208
 PAIRS = 64
 LATS = 128
 TWO_PI = 6.283185307179586
@@ -51,10 +52,10 @@
 
 
 def kernel(
-    mids_ref, bands_ref, nlon_ref, spec_ref, leg_ref, mrow_ref, out_ref,
-    spec_f, send_s, send_l, recv_s, recv_l, rhs, sums, send_r, recv_x,
+    mids_hbm, bands_hbm, nlon_hbm, spec_hbm, leg_hbm, mids_rows_hbm, out_ref,
+    mids_ref, bands_ref, nlon_ref, spec_ref, leg_ref, mids_rows, mrow_ref, spec_f, send_s, send_l, recv_s, recv_l, rhs, sums, send_r, recv_x,
     onehot, send_y, recv_z, zf, zs, expand, mcol, cosc, sinc, tw, mod, lat,
-    ss_send, ss_recv, sl_send, sl_recv, sx_send, sx_recv, sz_send, sz_recv,
+    load_sem, ss_send, ss_recv, sl_send, sl_recv, sx_send, sx_recv, sz_send, sz_recv,
 ):
     w = lax.axis_index("wave")
     me = lax.axis_index("lev")
@@ -63,17 +64,23 @@
     half = z // 4
 
     barrier = pltpu.get_barrier_semaphore()
-
-    def greet_lev(k, carry):
+    for k in range(1, LEVS):
         pl.semaphore_signal(barrier, inc=1, device_id={"lev": lax.rem(me + k, LEVS)}, device_id_type=MESH)
-        return carry
-
-    def greet_wave(k, carry):
+    for k in range(1, WAVES):
         pl.semaphore_signal(barrier, inc=1, device_id={"wave": lax.rem(w + k, WAVES)}, device_id_type=MESH)
-        return carry
-
-    lax.fori_loop(1, LEVS, greet_lev, 0)
-    lax.fori_loop(1, WAVES, greet_wave, 0)
+
+    mids_rows[...] = jnp.zeros_like(mids_rows)
+    loads = [
+        pltpu.make_async_copy(spec_hbm, spec_ref, load_sem.at[0]),
+        pltpu.make_async_copy(leg_hbm, leg_ref, load_sem.at[1]),
+        pltpu.make_async_copy(mids_rows_hbm, mids_rows.at[0:10], load_sem.at[2]),
+        pltpu.make_async_copy(mids_hbm, mids_ref, load_sem.at[3]),
+        pltpu.make_async_copy(bands_hbm, bands_ref, load_sem.at[4]),
+        pltpu.make_async_copy(nlon_hbm, nlon_ref, load_sem.at[5]),
+    ]
+    for load in loads:
+        load.start()
+    loads[0].wait()
 
     for tile in range(10):
         spec_f[tile, 0:240, :] = spec_ref[:, 128 * tile:128 * tile + 128].astype(F32)
@@ -84,20 +91,30 @@
         1.0, 0.0,
     ).astype(BF16)
 
+    fold = jnp.where(
+        (lax.broadcasted_iota(jnp.int32, (48, BLOCK), 0) == lax.broadcasted_iota(jnp.int32, (48, BLOCK), 1))
+        | (lax.broadcasted_iota(jnp.int32, (48, BLOCK), 0) + 40 == lax.broadcasted_iota(jnp.int32, (48, BLOCK), 1)),
+        1.0, 0.0,
+    )
+    fold = jnp.where(lax.broadcasted_iota(jnp.int32, (48, BLOCK), 0) < 40, fold, 0.0).astype(BF16)
+    upper = (lax.broadcasted_iota(jnp.int32, (LATS, BLOCK), 0) < PAIRS) == (
+        lax.broadcasted_iota(jnp.int32, (LATS, BLOCK), 1) < 40
+    )
+    loads[1].wait()
     pl.semaphore_wait(barrier, LEVS + WAVES - 2)
 
     def spec_copy(k, h):
         to = lax.rem(z + k, CHIPS)
         return pltpu.make_async_remote_copy(
-            src_ref=send_s.at[to, h], dst_ref=recv_s.at[me], send_sem=ss_send.at[2 * k + h],
-            recv_sem=ss_recv.at[me], device_id={"lev": 2 * to + h}, device_id_type=MESH,
+            src_ref=send_s.at[to, h], dst_ref=recv_s.at[me], send_sem=ss_send,
+            recv_sem=ss_recv, device_id={"lev": 2 * to + h}, device_id_type=MESH,
         )
 
     def leg_copy(k):
         to = lax.rem(z + k, CHIPS)
         return pltpu.make_async_remote_copy(
-            src_ref=send_l.at[to], dst_ref=recv_l.at[lax.rem(me, 8)], send_sem=sl_send.at[k],
-            recv_sem=sl_recv.at[lax.rem(me, 8)], device_id={"lev": 2 * to + half}, device_id_type=MESH,
+            src_ref=send_l.at[to], dst_ref=recv_l.at[lax.rem(me, 8)], send_sem=sl_send,
+            recv_sem=sl_recv, device_id={"lev": 2 * to + half}, device_id_type=MESH,
         )
 
     def prepare(k):
@@ -105,26 +122,27 @@
         for tile in range(10):
             rows = spec_f[tile, pl.ds(to, 32, stride=8), :].astype(BF16)
             send_s[to, tile // 5, :, 128 * (tile % 5):128 * (tile % 5) + 128] = rows
-        for p in range(3):
-            first = leg_ref[16 * p + to]
-            second = leg_ref[16 * p + 8 + to] if p < 2 else jnp.zeros((PAIRS, BLOCK), BF16)
-            stacked = jnp.concatenate([first, second], axis=0)
+        for p in range(2):
+            stacked = jnp.concatenate([leg_ref[16 * p + to], leg_ref[16 * p + 8 + to]], axis=0)
             send_l[to, BLOCK * p:BLOCK * p + BLOCK, :] = nt_dot(unit, stacked).astype(BF16)
+        last = leg_ref[32 + to].astype(F32)
+        stacked = jnp.where(upper, jnp.concatenate([last, last], axis=0), 0.0).astype(BF16)
+        send_l[to, 2 * BLOCK:LEG_ROWS, :] = nt_dot(fold, stacked).astype(BF16)
 
     def send_far(i, carry):
-        k = CHIPS - i
+        k = jnp.where(lax.rem(i, 2) == 1, 4 - (i + 1) // 2, 4 + i // 2)
         prepare(k)
         for h in range(2):
             spec_copy(k, h).start()
         leg_copy(k).start()
         return carry
 
-    lax.fori_loop(1, CHIPS, send_far, 0)
+    lax.fori_loop(0, CHIPS - 1, send_far, 0)
     prepare(0)
     for h in range(2):
         @pl.when(c == h)
         def _():
-            pltpu.make_async_copy(send_s.at[z, h], recv_s.at[me], ss_recv.at[me]).start()
+            pltpu.make_async_copy(send_s.at[z, h], recv_s.at[me], ss_recv).start()
 
         @pl.when(c != h)
         def _():
@@ -132,11 +150,14 @@
 
     @pl.when(c == half)
     def _():
-        pltpu.make_async_copy(send_l.at[z], recv_l.at[lax.rem(me, 8)], sl_recv.at[lax.rem(me, 8)]).start()
+        pltpu.make_async_copy(send_l.at[z], recv_l.at[lax.rem(me, 8)], sl_recv).start()
 
     @pl.when(c != half)
     def _():
         leg_copy(0).start()
+
+    for load in loads[2:]:
+        load.wait()
 
     start = jnp.int32(0)
     own_start = jnp.int32(0)
@@ -173,9 +194,21 @@
 
     lax.fori_loop(0, 20, fill_expand, 0)
 
+    natural = mids_rows[...].astype(F32)
+    high = jnp.floor(natural * 0.125)
+    digits = jnp.concatenate([high, natural - 8.0 * high], axis=0).astype(BF16)
     for t in range(10):
-        row = jnp.broadcast_to(mrow_ref[0:1, 128 * t:128 * t + 128], (128, 128))
-        mcol[128 * t:128 * t + 128, :] = row.T
+        place = lax.broadcasted_iota(jnp.int32, (128, 128), 1) + 128 * t
+        group = place >> 6
+        zl = jnp.where(group >= 5, 1, 0) + jnp.where(group >= 10, 1, 0) + jnp.where(group >= 15, 1, 0)
+        source = SLOTS * ((place & 63) >> 1) + 8 * (group - GROUP * zl) + 4 * (place & 1) + zl
+        pick = lax.broadcasted_iota(jnp.int32, (128, 128), 0) == (source & 127)
+        found = jnp.dot(digits, jnp.where(pick, 1.0, 0.0).astype(BF16), preferred_element_type=F32)
+        found = 8.0 * found[0:16, :] + found[16:32, :]
+        here = lax.broadcasted_iota(jnp.int32, (16, 128), 0) == (source[0:16, :] >> 7)
+        row = jnp.sum(jnp.where(here, found, 0.0), axis=0, keepdims=True)
+        mrow_ref[0:1, 128 * t:128 * t + 128] = row
+        mcol[128 * t:128 * t + 128, :] = jnp.broadcast_to(row, (128, 128)).T
 
     col1 = lax.broadcasted_iota(jnp.int32, (1, 128), 1)
     channel1 = jnp.where(col1 >= KH, 1, 0) + jnp.where(col1 >= 2 * KH, 1, 0)
@@ -217,16 +250,8 @@
 
     lax.fori_loop(0, LAT_MAX, tables, 0)
 
-    def wait_spec(k, carry):
-        pltpu.make_async_copy(recv_s.at[k], recv_s.at[k], ss_recv.at[k]).wait()
-        return carry
-
-    def wait_leg(k, carry):
-        pltpu.make_async_copy(recv_l.at[k], recv_l.at[k], sl_recv.at[k]).wait()
-        return carry
-
-    lax.fori_loop(0, LEVS, wait_spec, 0)
-    lax.fori_loop(0, 8, wait_leg, 0)
+    pltpu.make_async_copy(recv_s, recv_s, ss_recv).wait()
+    pltpu.make_async_copy(recv_l, recv_l, sl_recv).wait()
 
     left = recv_s[...].reshape(512, HALF)
     row_r = lax.broadcasted_iota(jnp.int32, (512, 256), 0) & 31
@@ -238,7 +263,12 @@
         m_a = mids_ref[SLOTS * w + 16 * p + z]
         m_b = mids_ref[SLOTS * w + 16 * p + 8 + z] if p < 2 else m_a
         m = jnp.where(lane_n < PAIRS, m_a, m_b)
-        table = recv_l[:, BLOCK * p:BLOCK * p + BLOCK, :].reshape(HALF, 128).astype(F32)
+        if p < 2:
+            table = recv_l[:, BLOCK * p:BLOCK * p + BLOCK, :].astype(F32).reshape(HALF, 128)
+        else:
+            packed = recv_l[:, 2 * BLOCK:LEG_ROWS, :].astype(F32)
+            swapped = jnp.concatenate([packed[:, :, 64:128], packed[:, :, 0:64]], axis=2)
+            table = jnp.concatenate([packed[:, 0:40], swapped[:, 0:40]], axis=1).reshape(HALF, 128)
         table = jnp.where(degree >= m, table, 0.0)
         rhs[:, 0:128] = table.astype(BF16)
         rhs[:, 128:256] = jnp.where(((degree + m) & 1) == 1, -table, table).astype(BF16)
@@ -253,22 +283,14 @@
     def level_copy(k):
         to = lax.rem(me + k, LEVS)
         return pltpu.make_async_remote_copy(
-            src_ref=send_r.at[to], dst_ref=recv_x.at[me], send_sem=sx_send.at[k],
-            recv_sem=sx_recv.at[me], device_id={"lev": to}, device_id_type=MESH,
+            src_ref=send_r.at[to], dst_ref=recv_x.at[me], send_sem=sx_send,
+            recv_sem=sx_recv, device_id={"lev": to}, device_id_type=MESH,
         )
 
-    def send_level(k, carry):
+    for k in sorted(range(1, LEVS), key=lambda k: abs(k - LEVS // 2)):
         level_copy(k).start()
-        return carry
-
-    lax.fori_loop(1, LEVS, send_level, 0)
-    pltpu.make_async_copy(send_r.at[me], recv_x.at[me], sx_recv.at[me]).start()
-
-    def wait_level(k, carry):
-        pltpu.make_async_copy(recv_x.at[k], recv_x.at[k], sx_recv.at[k]).wait()
-        return carry
-
-    lax.fori_loop(0, LEVS, wait_level, 0)
+    pltpu.make_async_copy(send_r.at[me], recv_x.at[me], sx_recv).start()
+    pltpu.make_async_copy(recv_x, recv_x, sx_recv).wait()
 
     got = recv_x[...].astype(F32).reshape(CHIPS, 2, 32, 256)
     level_sums = (got[:, 0] + got[:, 1]).reshape(256, 256).astype(BF16)
@@ -280,22 +302,14 @@
     def band_copy(k):
         to = lax.rem(w + k, WAVES)
         return pltpu.make_async_remote_copy(
-            src_ref=send_y.at[to], dst_ref=recv_z.at[w], send_sem=sz_send.at[k],
-            recv_sem=sz_recv.at[w], device_id={"wave": to}, device_id_type=MESH,
+            src_ref=send_y.at[to], dst_ref=recv_z.at[w], send_sem=sz_send,
+            recv_sem=sz_recv, device_id={"wave": to}, device_id_type=MESH,
         )
 
-    def send_band(k, carry):
+    for k in sorted(range(1, WAVES), key=lambda k: abs(k - WAVES // 2)):
         band_copy(k).start()
-        return carry
-
-    lax.fori_loop(1, WAVES, send_band, 0)
-    pltpu.make_async_copy(send_y.at[w], recv_z.at[w], sz_recv.at[w]).start()
-
-    def wait_band(k, carry):
-        pltpu.make_async_copy(recv_z.at[k], recv_z.at[k], sz_recv.at[k]).wait()
-        return carry
-
-    lax.fori_loop(0, WAVES, wait_band, 0)
+    pltpu.make_async_copy(send_y.at[w], recv_z.at[w], sz_recv).start()
+    pltpu.make_async_copy(recv_z, recv_z, sz_recv).wait()
 
     zf[...] = recv_z[...].astype(F32).reshape(512, 128)
     for slot in range(LAT_MAX):
@@ -335,53 +349,48 @@
             tile = jnp.where(lon + 128 * kh < cycles, lat[at:at + 8, :], 0.0).astype(BF16)
             out_ref[f, :, 128 * kh:128 * kh + width] = tile[:, 0:width]
 
-    def sent_far(k, carry):
-        for h in range(2):
-            spec_copy(k, h).wait_send()
-        leg_copy(k).wait_send()
-        return carry
-
-    lax.fori_loop(1, CHIPS, sent_far, 0)
-    for h in range(2):
-        @pl.when(c != h)
-        def _():
-            spec_copy(0, h).wait_send()
+    def all_sent(block, count, sem):
+        part = block.at[pl.ds(0, count)]
+        pltpu.make_async_copy(part, part, sem).wait()
+
+    all_sent(recv_s, LEVS - 1, ss_send)
+
+    @pl.when(c == half)
+    def _():
+        all_sent(recv_l, CHIPS - 1, sl_send)
 
     @pl.when(c != half)
     def _():
-        leg_copy(0).wait_send()
-
-    def sent_level(k, carry):
-        level_copy(k).wait_send()
-        return carry
-
-    lax.fori_loop(1, LEVS, sent_level, 0)
-
-    def sent_band(k, carry):
-        band_copy(k).wait_send()
-        return carry
-
-    lax.fori_loop(1, WAVES, sent_band, 0)
+        all_sent(recv_l, CHIPS, sl_send)
+
+    all_sent(recv_x, LEVS - 1, sx_send)
+    all_sent(recv_z, WAVES - 1, sz_send)
 
 
 def on_device(spec, legendre, mids, band_lats, nlon):
     spec_rows = spec.reshape(240, MW)
     tables = jnp.transpose(legendre, (0, 2, 1))
-    order = jnp.transpose(mids.reshape(WAVES, GROUP, 2, 4), (3, 1, 0, 2)).reshape(1, MW).astype(F32)
-    smem = pl.BlockSpec(memory_space=pltpu.SMEM)
+    hbm = pl.BlockSpec(memory_space=pltpu.HBM)
     vmem = pl.BlockSpec(memory_space=pltpu.VMEM)
     dma = pltpu.SemaphoreType.DMA
     planes = pl.pallas_call(
         kernel,
         out_shape=jax.ShapeDtypeStruct((3, LAT_MAX, NLON_MAX), BF16),
-        in_specs=[smem, smem, smem, vmem, vmem, vmem],
+        in_specs=[hbm] * 6,
         out_specs=vmem,
         scratch_shapes=[
+            pltpu.SMEM((MW,), jnp.int32),
+            pltpu.SMEM((WAVES,), jnp.int32),
+            pltpu.SMEM((PAIRS,), jnp.int32),
+            pltpu.VMEM((240, MW), BF16),
+            pltpu.VMEM((SLOTS, PAIRS, BLOCK), BF16),
+            pltpu.VMEM((16, 128), jnp.int32),
+            pltpu.VMEM((1, MW), F32),
             pltpu.VMEM((10, 256, 128), F32),
             pltpu.VMEM((CHIPS, 2, 32, HALF), BF16),
-            pltpu.VMEM((CHIPS, 3 * BLOCK, 128), BF16),
+            pltpu.VMEM((CHIPS, LEG_ROWS, 128), BF16),
             pltpu.VMEM((LEVS, 32, HALF), BF16),
-            pltpu.VMEM((8, 3 * BLOCK, 128), BF16),
+            pltpu.VMEM((8, LEG_ROWS, 128), BF16),
             pltpu.VMEM((HALF, 256), BF16),
             pltpu.VMEM((512, 256), F32),
             pltpu.VMEM((LEVS, 32, 256), BF16),
@@ -398,13 +407,12 @@
             pltpu.VMEM((LAT_MAX, 128, 2 * MW), BF16),
             pltpu.VMEM((LAT_MAX, 2 * MW, 128), BF16),
             pltpu.VMEM((1024, 128), F32),
-            dma((2 * CHIPS,)), dma((LEVS,)), dma((CHIPS,)), dma((8,)),
-            dma((LEVS,)), dma((LEVS,)), dma((WAVES,)), dma((WAVES,)),
+            dma((6,)), dma, dma, dma, dma, dma, dma, dma, dma,
         ],
         compiler_params=pltpu.CompilerParams(
-            collective_id=0, has_side_effects=True, vmem_limit_bytes=52 * 2**20
+            collective_id=0, has_side_effects=True, vmem_limit_bytes=58 * 2**20
         ),
-    )(mids, band_lats, nlon, spec_rows, tables, order)
+    )(mids, band_lats, nlon, spec_rows, tables, mids.reshape(10, 128))
     return jnp.transpose(planes, (1, 0, 2)).reshape(LAT_MAX, 3, 1, NLON_MAX)
 
 

time: 74.6 us -> 65.5 us (0.88)
  Pallas kernels: 69.6 us -> 63.7 us
  local copies, waits for them, and re-layouts: 3.97 us -> 1.66 us
  other arithmetic: 0.76 us -> 0 us
    pallas_call x1, Pallas kernels: 69.6 us -> 63.7 us  [on_device(): pl.pallas_call(kernel, out_shape=jax.ShapeDtypeStruct((3, LAT_MAX, NLON_M...]
    convert_element_type x3 -> x0, local copies, waits for them, and re-layouts: 1.73 us -> none  [on_device(): jnp.transpose(mids.reshape(WAVES, GROUP, 2, 4), (3, 1, 0, 2)).reshape(1, MW)]
    convert_element_type x1 -> x0, other arithmetic: 0.76 us -> none  [on_device(): jnp.transpose(mids.reshape(WAVES, GROUP, 2, 4), (3, 1, 0, 2)).reshape(1, MW)]
    unnamed x11 -> x1, local copies, waits for them, and re-layouts: 2.24 us -> 1.66 us
where the time goes in v1:
time: 65.5 us; the launch traced here: 65.3 us
  Pallas kernels  63.7 us (97%)
  local copies, waits for them, and re-layouts  1.66 us (3%)
    pallas_call x1, Pallas kernels, on_device(): pl.pallas_call(kernel, out_shape=jax.ShapeDtypeStruct((3, LAT_MAX, NLON_M...  63.7 us
    unnamed x1, local copies, waits for them, and re-layouts  1.66 us

profile of v1, /device:TPU:1, one launch (start us, length us, event | category | flops | bytes accessed | tf_op | source)
XLA Modules:
  0.0 65.3 jit_solution(3718630868653439960)
XLA Ops:
  0.0 63.7 %shard_map.55 = bf16[3,8,5136]{2,1,0:T(8,128)(2,1)} custom-call(s32[1280]{0:T(1024)} %mids_hbm.1, s32[32]{0:T(128)} %bands_hbm.1, s32[64]{0:T(128)} %nlon_hbm.1, bf16[240,1280]{1,0:T(8,128)(2,1)} %bitcast.10, bf16[40,64,80]{2,1,0:T(8,128)(2,1)} %bitcast.9, s32[10,128]{1,0:T(8,128)} %bitcast.11), custom_call_target="tpu_custom_call" | custom-call | tf_op jit(solution)/shard_map/pallas_call | solution.py:376
  63.7 1.7 %copy.8 = bf16[8,3,1,5136]{3,0,2,1:T(8,128)(2,1)} copy(bf16[8,3,1,5136]{3,0,2,1:T(8,128)(2,1)} %bitcast.8) | data formatting | bytes 493056

commit v2 on v1

--- a/solution.py
+++ b/solution.py
@@ -161,9 +161,9 @@
 
     start = jnp.int32(0)
     own_start = jnp.int32(0)
-    sub16 = lax.broadcasted_iota(jnp.int32, (16, 256), 0)
-    lane = lax.broadcasted_iota(jnp.int32, (16, 256), 1)
-    lat_of = jnp.where(lane < 128, lane & 63, 127 - (lane & 63))
+    sub16 = lax.broadcasted_iota(jnp.int32, (16, 128), 0)
+    lane = lax.broadcasted_iota(jnp.int32, (16, 128), 1)
+    lat_of = jnp.where(lane < PAIRS, lane, LATS - 1 - (lane - PAIRS))
     for e in range(WAVES // 2):
         count_a, count_b = bands_ref[2 * e], bands_ref[2 * e + 1]
         start_b = start + count_a
@@ -277,8 +277,12 @@
             sums[...] = terms
         else:
             sums[...] = jnp.where(j_r >= 2 * p, terms, sums[...])
-    keep = ((lane_r & 127) < PAIRS) == ((j_r & 1) == 0)
-    send_r[...] = jnp.where(keep, sums[...], 0.0).astype(BF16).reshape(LEVS, 32, 256)
+    north, south = sums[:, 0:128], sums[:, 128:256]
+    odd = (j_r[:, 0:128] & 1) == 1
+    north = jnp.where(odd, pltpu.roll(north, PAIRS, 1), north)
+    south = jnp.where(odd, south, pltpu.roll(south, PAIRS, 1))
+    both_halves = jnp.where(lane_r[:, 0:128] < PAIRS, north, south)
+    send_r[...] = both_halves.astype(BF16).reshape(LEVS, 32, 128)
 
     def level_copy(k):
         to = lax.rem(me + k, LEVS)
@@ -292,8 +296,8 @@
     pltpu.make_async_copy(send_r.at[me], recv_x.at[me], sx_recv).start()
     pltpu.make_async_copy(recv_x, recv_x, sx_recv).wait()
 
-    got = recv_x[...].astype(F32).reshape(CHIPS, 2, 32, 256)
-    level_sums = (got[:, 0] + got[:, 1]).reshape(256, 256).astype(BF16)
+    got = recv_x[...].astype(F32).reshape(CHIPS, 2, 32, 128)
+    level_sums = (got[:, 0] + got[:, 1]).reshape(256, 128).astype(BF16)
     by_slot = nt_dot(onehot[...], level_sums)
     low = by_slot[:, 0:128].reshape(WAVES, 8, 128)
     high = by_slot[:, 128:256].reshape(WAVES, 8, 128)
@@ -393,9 +397,9 @@
             pltpu.VMEM((8, LEG_ROWS, 128), BF16),
             pltpu.VMEM((HALF, 256), BF16),
             pltpu.VMEM((512, 256), F32),
-            pltpu.VMEM((LEVS, 32, 256), BF16),
-            pltpu.VMEM((LEVS, 32, 256), BF16),
-            pltpu.VMEM((256, 256), BF16),
+            pltpu.VMEM((LEVS, 32, 128), BF16),
+            pltpu.VMEM((LEVS, 32, 128), BF16),
+            pltpu.VMEM((256, 128), BF16),
             pltpu.VMEM((WAVES, 16, 128), BF16),
             pltpu.VMEM((WAVES, 16, 128), BF16),
             pltpu.VMEM((512, 128), F32),

time: 65.5 us -> 64 us (0.977)
  Pallas kernels: 63.7 us -> 62.1 us
    pallas_call x1, Pallas kernels: 63.7 us -> 62.1 us  [on_device(): pl.pallas_call(kernel, out_shape=jax.ShapeDtypeStruct((3, LAT_MAX, NLON_M...]
where the time goes in v2:
time: 64 us; the launch traced here: 63.8 us
  Pallas kernels  62.1 us (97%)
  local copies, waits for them, and re-layouts  1.66 us (3%)
    pallas_call x1, Pallas kernels, on_device(): pl.pallas_call(kernel, out_shape=jax.ShapeDtypeStruct((3, LAT_MAX, NLON_M...  62.1 us
    unnamed x1, local copies, waits for them, and re-layouts  1.66 us

profile of v2, /device:TPU:1, one launch (start us, length us, event | category | flops | bytes accessed | tf_op | source)
XLA Modules:
  0.0 63.8 jit_solution(18382058224801751585)
XLA Ops:
  0.0 62.1 %shard_map.55 = bf16[3,8,5136]{2,1,0:T(8,128)(2,1)} custom-call(s32[1280]{0:T(1024)} %mids_hbm.1, s32[32]{0:T(128)} %bands_hbm.1, s32[64]{0:T(128)} %nlon_hbm.1, bf16[240,1280]{1,0:T(8,128)(2,1)} %bitcast.10, bf16[40,64,80]{2,1,0:T(8,128)(2,1)} %bitcast.9, s32[10,128]{1,0:T(8,128)} %bitcast.11), custom_call_target="tpu_custom_call" | custom-call | tf_op jit(solution)/shard_map/pallas_call | solution.py:380
  62.1 1.7 %copy.8 = bf16[8,3,1,5136]{3,0,2,1:T(8,128)(2,1)} copy(bf16[8,3,1,5136]{3,0,2,1:T(8,128)(2,1)} %bitcast.8) | data formatting | bytes 493056

commit v3 on v2

--- a/solution.py
+++ b/solution.py
@@ -53,7 +53,7 @@
 
 def kernel(
     mids_hbm, bands_hbm, nlon_hbm, spec_hbm, leg_hbm, mids_rows_hbm, out_ref,
-    mids_ref, bands_ref, nlon_ref, spec_ref, leg_ref, mids_rows, mrow_ref, spec_f, send_s, send_l, recv_s, recv_l, rhs, sums, send_r, recv_x,
+    mids_ref, bands_ref, nlon_ref, spec_ref, leg_ref, mids_rows, mrow_ref, spec_f, send_s, send_l, recv_s, recv_l, rhs, slot_j, send_r, recv_x,
     onehot, send_y, recv_z, zf, zs, expand, mcol, cosc, sinc, tw, mod, lat,
     load_sem, ss_send, ss_recv, sl_send, sl_recv, sx_send, sx_recv, sz_send, sz_recv,
 ):
@@ -63,16 +63,10 @@
     c = me - 2 * z
     half = z // 4
 
-    barrier = pltpu.get_barrier_semaphore()
-    for k in range(1, LEVS):
-        pl.semaphore_signal(barrier, inc=1, device_id={"lev": lax.rem(me + k, LEVS)}, device_id_type=MESH)
-    for k in range(1, WAVES):
-        pl.semaphore_signal(barrier, inc=1, device_id={"wave": lax.rem(w + k, WAVES)}, device_id_type=MESH)
-
     mids_rows[...] = jnp.zeros_like(mids_rows)
     loads = [
-        pltpu.make_async_copy(spec_hbm, spec_ref, load_sem.at[0]),
-        pltpu.make_async_copy(leg_hbm, leg_ref, load_sem.at[1]),
+        pltpu.make_async_copy(leg_hbm, leg_ref, load_sem.at[0]),
+        pltpu.make_async_copy(spec_hbm, spec_ref, load_sem.at[1]),
         pltpu.make_async_copy(mids_rows_hbm, mids_rows.at[0:10], load_sem.at[2]),
         pltpu.make_async_copy(mids_hbm, mids_ref, load_sem.at[3]),
         pltpu.make_async_copy(bands_hbm, bands_ref, load_sem.at[4]),
@@ -80,11 +74,13 @@
     ]
     for load in loads:
         load.start()
-    loads[0].wait()
-
-    for tile in range(10):
-        spec_f[tile, 0:240, :] = spec_ref[:, 128 * tile:128 * tile + 128].astype(F32)
-        spec_f[tile, 240:256, :] = jnp.zeros((16, 128), F32)
+
+    barrier = pltpu.get_barrier_semaphore()
+    for k in range(1, LEVS):
+        pl.semaphore_signal(barrier, inc=1, device_id={"lev": lax.rem(me + k, LEVS)}, device_id_type=MESH)
+    for k in range(1, WAVES):
+        pl.semaphore_signal(barrier, inc=1, device_id={"wave": lax.rem(w + k, WAVES)}, device_id_type=MESH)
+
 
     unit = jnp.where(
         lax.broadcasted_iota(jnp.int32, (BLOCK, BLOCK), 0) == lax.broadcasted_iota(jnp.int32, (BLOCK, BLOCK), 1),
@@ -100,7 +96,7 @@
     upper = (lax.broadcasted_iota(jnp.int32, (LATS, BLOCK), 0) < PAIRS) == (
         lax.broadcasted_iota(jnp.int32, (LATS, BLOCK), 1) < 40
     )
-    loads[1].wait()
+    loads[0].wait()
     pl.semaphore_wait(barrier, LEVS + WAVES - 2)
 
     def spec_copy(k, h):
@@ -117,11 +113,11 @@
             recv_sem=sl_recv, device_id={"lev": 2 * to + half}, device_id_type=MESH,
         )
 
-    def prepare(k):
+    def order_of(i):
+        return jnp.where(lax.rem(i, 2) == 1, 4 - (i + 1) // 2, 4 + i // 2)
+
+    def prepare_leg(k):
         to = lax.rem(z + k, CHIPS)
-        for tile in range(10):
-            rows = spec_f[tile, pl.ds(to, 32, stride=8), :].astype(BF16)
-            send_s[to, tile // 5, :, 128 * (tile % 5):128 * (tile % 5) + 128] = rows
         for p in range(2):
             stacked = jnp.concatenate([leg_ref[16 * p + to], leg_ref[16 * p + 8 + to]], axis=0)
             send_l[to, BLOCK * p:BLOCK * p + BLOCK, :] = nt_dot(unit, stacked).astype(BF16)
@@ -129,16 +125,43 @@
         stacked = jnp.where(upper, jnp.concatenate([last, last], axis=0), 0.0).astype(BF16)
         send_l[to, 2 * BLOCK:LEG_ROWS, :] = nt_dot(fold, stacked).astype(BF16)
 
-    def send_far(i, carry):
-        k = jnp.where(lax.rem(i, 2) == 1, 4 - (i + 1) // 2, 4 + i // 2)
-        prepare(k)
+    def prepare_spec(k):
+        to = lax.rem(z + k, CHIPS)
+        for tile in range(10):
+            rows = spec_f[tile, pl.ds(to, 32, stride=8), :].astype(BF16)
+            send_s[to, tile // 5, :, 128 * (tile % 5):128 * (tile % 5) + 128] = rows
+
+    def send_leg(i, carry):
+        k = order_of(i)
+        prepare_leg(k)
+        leg_copy(k).start()
+        return carry
+
+    lax.fori_loop(0, CHIPS - 1, send_leg, 0)
+    prepare_leg(0)
+
+    @pl.when(c == half)
+    def _():
+        pltpu.make_async_copy(send_l.at[z], recv_l.at[lax.rem(me, 8)], sl_recv).start()
+
+    @pl.when(c != half)
+    def _():
+        leg_copy(0).start()
+
+    loads[1].wait()
+    for tile in range(10):
+        spec_f[tile, 0:240, :] = spec_ref[:, 128 * tile:128 * tile + 128].astype(F32)
+        spec_f[tile, 240:256, :] = jnp.zeros((16, 128), F32)
+
+    def send_spec(i, carry):
+        k = order_of(i)
+        prepare_spec(k)
         for h in range(2):
             spec_copy(k, h).start()
-        leg_copy(k).start()
-        return carry
-
-    lax.fori_loop(0, CHIPS - 1, send_far, 0)
-    prepare(0)
+        return carry
+
+    lax.fori_loop(0, CHIPS - 1, send_spec, 0)
+    prepare_spec(0)
     for h in range(2):
         @pl.when(c == h)
         def _():
@@ -147,14 +170,6 @@
         @pl.when(c != h)
         def _():
             spec_copy(0, h).start()
-
-    @pl.when(c == half)
-    def _():
-        pltpu.make_async_copy(send_l.at[z], recv_l.at[lax.rem(me, 8)], sl_recv).start()
-
-    @pl.when(c != half)
-    def _():
-        leg_copy(0).start()
 
     for load in loads[2:]:
         load.wait()
@@ -250,13 +265,7 @@
 
     lax.fori_loop(0, LAT_MAX, tables, 0)
 
-    pltpu.make_async_copy(recv_s, recv_s, ss_recv).wait()
     pltpu.make_async_copy(recv_l, recv_l, sl_recv).wait()
-
-    left = recv_s[...].reshape(512, HALF)
-    row_r = lax.broadcasted_iota(jnp.int32, (512, 256), 0) & 31
-    j_r = row_r - GROUP * jnp.floor((row_r.astype(F32) + 0.5) * 0.2).astype(jnp.int32)
-    lane_r = lax.broadcasted_iota(jnp.int32, (512, 256), 1)
     degree = lax.broadcasted_iota(jnp.int32, (HALF, 128), 0) + HALF * c
     lane_n = lax.broadcasted_iota(jnp.int32, (HALF, 128), 1)
     for p in range(3):
@@ -270,18 +279,26 @@
             swapped = jnp.concatenate([packed[:, :, 64:128], packed[:, :, 0:64]], axis=2)
             table = jnp.concatenate([packed[:, 0:40], swapped[:, 0:40]], axis=1).reshape(HALF, 128)
         table = jnp.where(degree >= m, table, 0.0)
-        rhs[:, 0:128] = table.astype(BF16)
-        rhs[:, 128:256] = jnp.where(((degree + m) & 1) == 1, -table, table).astype(BF16)
-        terms = jnp.dot(left, rhs[...], preferred_element_type=F32)
-        if p == 0:
-            sums[...] = terms
-        else:
-            sums[...] = jnp.where(j_r >= 2 * p, terms, sums[...])
-    north, south = sums[:, 0:128], sums[:, 128:256]
-    odd = (j_r[:, 0:128] & 1) == 1
+        rhs[p, :, 0:128] = table.astype(BF16)
+        rhs[p, :, 128:256] = jnp.where(((degree + m) & 1) == 1, -table, table).astype(BF16)
+
+    row_r = lax.broadcasted_iota(jnp.int32, (512, 128), 0) & 31
+    j_r = row_r - GROUP * jnp.floor((row_r.astype(F32) + 0.5) * 0.2).astype(jnp.int32)
+    slot_j[...] = j_r
+    lane_r = lax.broadcasted_iota(jnp.int32, (32, 128), 1)
+    pltpu.make_async_copy(recv_s, recv_s, ss_recv).wait()
+
+    left = recv_s[...].reshape(512, HALF)
+    terms = [jnp.dot(left, rhs[p], preferred_element_type=F32) for p in range(3)]
+    j_r = slot_j[...]
+    north, south = [
+        jnp.where(j_r >= 4, terms[2][:, at:at + 128], jnp.where(j_r >= 2, terms[1][:, at:at + 128], terms[0][:, at:at + 128]))
+        for at in (0, 128)
+    ]
+    odd = (j_r & 1) == 1
     north = jnp.where(odd, pltpu.roll(north, PAIRS, 1), north)
     south = jnp.where(odd, south, pltpu.roll(south, PAIRS, 1))
-    both_halves = jnp.where(lane_r[:, 0:128] < PAIRS, north, south)
+    both_halves = jnp.where(lane_r[0:1, :] < PAIRS, north, south)
     send_r[...] = both_halves.astype(BF16).reshape(LEVS, 32, 128)
 
     def level_copy(k):
@@ -332,14 +349,14 @@
             mod[slot, pl.ds(other, 64), :] = (re * sin_part + im * cos_part).astype(BF16)
         return carry
 
-    lax.fori_loop(0, 20, modulate, 0)
+    lax.fori_loop(0, 20, modulate, 0, unroll=20)
 
     def transform(slot, carry):
         points = jnp.dot(tw[slot], mod[slot], preferred_element_type=F32)
         lat[pl.ds(slot, 128, stride=8), :] = points.T
         return carry
 
-    lax.fori_loop(0, LAT_MAX, transform, 0)
+    lax.fori_loop(0, LAT_MAX, transform, 0, unroll=8)
 
     slot_of = lax.broadcasted_iota(jnp.int32, (8, 128), 0)
     lon = lax.broadcasted_iota(jnp.int32, (8, 128), 1)
@@ -395,8 +412,8 @@
             pltpu.VMEM((CHIPS, LEG_ROWS, 128), BF16),
             pltpu.VMEM((LEVS, 32, HALF), BF16),
             pltpu.VMEM((8, LEG_ROWS, 128), BF16),
-            pltpu.VMEM((HALF, 256), BF16),
-            pltpu.VMEM((512, 256), F32),
+            pltpu.VMEM((3, HALF, 256), BF16),
+            pltpu.VMEM((512, 128), jnp.int32),
             pltpu.VMEM((LEVS, 32, 128), BF16),
             pltpu.VMEM((LEVS, 32, 128), BF16),
             pltpu.VMEM((256, 128), BF16),

time: 64 us -> 59.8 us (0.934)
  Pallas kernels: 62.1 us -> 58 us
    pallas_call x1, Pallas kernels: 62.1 us -> 58 us  [on_device(): pl.pallas_call(kernel, out_shape=jax.ShapeDtypeStruct((3, LAT_MAX, NLON_M...]
where the time goes in v3:
time: 59.8 us; the launch traced here: 59.7 us
  Pallas kernels  58 us (97%)
  local copies, waits for them, and re-layouts  1.66 us (3%)
    pallas_call x1, Pallas kernels, on_device(): pl.pallas_call(kernel, out_shape=jax.ShapeDtypeStruct((3, LAT_MAX, NLON_M...  58 us
    unnamed x1, local copies, waits for them, and re-layouts  1.66 us

profile of v3, /device:TPU:1, one launch (start us, length us, event | category | flops | bytes accessed | tf_op | source)
XLA Modules:
  0.0 59.7 jit_solution(6552548066178737414)
XLA Ops:
  0.0 58.0 %shard_map.55 = bf16[3,8,5136]{2,1,0:T(8,128)(2,1)} custom-call(s32[1280]{0:T(1024)} %mids_hbm.1, s32[32]{0:T(128)} %bands_hbm.1, s32[64]{0:T(128)} %nlon_hbm.1, bf16[240,1280]{1,0:T(8,128)(2,1)} %bitcast.10, bf16[40,64,80]{2,1,0:T(8,128)(2,1)} %bitcast.9, s32[10,128]{1,0:T(8,128)} %bitcast.11), custom_call_target="tpu_custom_call" | custom-call | tf_op jit(solution)/shard_map/pallas_call | solution.py:397
  58.0 1.7 %copy.8 = bf16[8,3,1,5136]{3,0,2,1:T(8,128)(2,1)} copy(bf16[8,3,1,5136]{3,0,2,1:T(8,128)(2,1)} %bitcast.8) | data formatting | bytes 493056

commit v4 on v3

--- a/solution.py
+++ b/solution.py
@@ -14,7 +14,6 @@
 SLOTS = 40
 GROUP = 5
 MW = 1280
-HALF = 640
 BLOCK = 80
 LEG_ROWS = 208
 PAIRS = 64
@@ -55,13 +54,12 @@
     mids_hbm, bands_hbm, nlon_hbm, spec_hbm, leg_hbm, mids_rows_hbm, out_ref,
     mids_ref, bands_ref, nlon_ref, spec_ref, leg_ref, mids_rows, mrow_ref, spec_f, send_s, send_l, recv_s, recv_l, rhs, slot_j, send_r, recv_x,
     onehot, send_y, recv_z, zf, zs, expand, mcol, cosc, sinc, tw, mod, lat,
-    load_sem, ss_send, ss_recv, sl_send, sl_recv, sx_send, sx_recv, sz_send, sz_recv,
+    load_sem, ss_send, ss_recv, sl_send, sl_recv, sf_send, sf_recv, sx_send, sx_recv, sz_send, sz_recv,
 ):
     w = lax.axis_index("wave")
     me = lax.axis_index("lev")
     z = me // 2
     c = me - 2 * z
-    half = z // 4
 
     mids_rows[...] = jnp.zeros_like(mids_rows)
     loads = [
@@ -76,8 +74,11 @@
         load.start()
 
     barrier = pltpu.get_barrier_semaphore()
-    for k in range(1, LEVS):
-        pl.semaphore_signal(barrier, inc=1, device_id={"lev": lax.rem(me + k, LEVS)}, device_id_type=MESH)
+    for k in sorted(range(1, CHIPS), key=lambda k: abs(k - CHIPS // 2)):
+        peer = 2 * lax.rem(z + k, CHIPS) + c
+        pl.semaphore_signal(barrier, inc=1, device_id={"lev": peer}, device_id_type=MESH)
+    sibling = 2 * z + (1 - c)
+    pl.semaphore_signal(barrier, inc=1, device_id={"lev": sibling}, device_id_type=MESH)
     for k in range(1, WAVES):
         pl.semaphore_signal(barrier, inc=1, device_id={"wave": lax.rem(w + k, WAVES)}, device_id_type=MESH)
 
@@ -97,20 +98,26 @@
         lax.broadcasted_iota(jnp.int32, (LATS, BLOCK), 1) < 40
     )
     loads[0].wait()
-    pl.semaphore_wait(barrier, LEVS + WAVES - 2)
-
-    def spec_copy(k, h):
+    pl.semaphore_wait(barrier, CHIPS + WAVES - 1)
+
+    def spec_copy(k):
         to = lax.rem(z + k, CHIPS)
         return pltpu.make_async_remote_copy(
-            src_ref=send_s.at[to, h], dst_ref=recv_s.at[me], send_sem=ss_send,
-            recv_sem=ss_recv, device_id={"lev": 2 * to + h}, device_id_type=MESH,
+            src_ref=send_s.at[to], dst_ref=recv_s.at[z], send_sem=ss_send,
+            recv_sem=ss_recv, device_id={"lev": 2 * to + c}, device_id_type=MESH,
         )
 
     def leg_copy(k):
         to = lax.rem(z + k, CHIPS)
         return pltpu.make_async_remote_copy(
-            src_ref=send_l.at[to], dst_ref=recv_l.at[lax.rem(me, 8)], send_sem=sl_send,
-            recv_sem=sl_recv, device_id={"lev": 2 * to + half}, device_id_type=MESH,
+            src_ref=send_l.at[to], dst_ref=recv_l.at[c, z], send_sem=sl_send,
+            recv_sem=sl_recv.at[z], device_id={"lev": 2 * to + c}, device_id_type=MESH,
+        )
+
+    def share_copy(chip):
+        return pltpu.make_async_remote_copy(
+            src_ref=recv_l.at[c, chip], dst_ref=recv_l.at[c, chip], send_sem=sf_send,
+            recv_sem=sf_recv, device_id={"lev": sibling}, device_id_type=MESH,
         )
 
     def order_of(i):
@@ -129,7 +136,7 @@
         to = lax.rem(z + k, CHIPS)
         for tile in range(10):
             rows = spec_f[tile, pl.ds(to, 32, stride=8), :].astype(BF16)
-            send_s[to, tile // 5, :, 128 * (tile % 5):128 * (tile % 5) + 128] = rows
+            send_s[to, :, 128 * tile:128 * tile + 128] = rows
 
     def send_leg(i, carry):
         k = order_of(i)
@@ -140,13 +147,7 @@
     lax.fori_loop(0, CHIPS - 1, send_leg, 0)
     prepare_leg(0)
 
-    @pl.when(c == half)
-    def _():
-        pltpu.make_async_copy(send_l.at[z], recv_l.at[lax.rem(me, 8)], sl_recv).start()
-
-    @pl.when(c != half)
-    def _():
-        leg_copy(0).start()
+    pltpu.make_async_copy(send_l.at[z], recv_l.at[c, z], sl_recv.at[z]).start()
 
     loads[1].wait()
     for tile in range(10):
@@ -156,20 +157,12 @@
     def send_spec(i, carry):
         k = order_of(i)
         prepare_spec(k)
-        for h in range(2):
-            spec_copy(k, h).start()
+        spec_copy(k).start()
         return carry
 
     lax.fori_loop(0, CHIPS - 1, send_spec, 0)
     prepare_spec(0)
-    for h in range(2):
-        @pl.when(c == h)
-        def _():
-            pltpu.make_async_copy(send_s.at[z, h], recv_s.at[me], ss_recv).start()
-
-        @pl.when(c != h)
-        def _():
-            spec_copy(0, h).start()
+    pltpu.make_async_copy(send_s.at[z], recv_s.at[z], ss_recv).start()
 
     for load in loads[2:]:
         load.wait()
@@ -265,30 +258,40 @@
 
     lax.fori_loop(0, LAT_MAX, tables, 0)
 
-    pltpu.make_async_copy(recv_l, recv_l, sl_recv).wait()
-    degree = lax.broadcasted_iota(jnp.int32, (HALF, 128), 0) + HALF * c
-    lane_n = lax.broadcasted_iota(jnp.int32, (HALF, 128), 1)
+    def share(i, carry):
+        chip = lax.rem(z - jnp.where(i == CHIPS - 1, 0, order_of(i)) + CHIPS, CHIPS)
+        pltpu.make_async_copy(recv_l.at[c, chip], recv_l.at[c, chip], sl_recv.at[chip]).wait()
+        share_copy(chip).start()
+        return carry
+
+    lax.fori_loop(0, CHIPS, share, 0)
+    pltpu.make_async_copy(recv_l.at[1 - c], recv_l.at[1 - c], sf_recv).wait()
+    degree = lax.broadcasted_iota(jnp.int32, (MW, 128), 0)
+    lane_n = lax.broadcasted_iota(jnp.int32, (MW, 128), 1)
     for p in range(3):
         m_a = mids_ref[SLOTS * w + 16 * p + z]
         m_b = mids_ref[SLOTS * w + 16 * p + 8 + z] if p < 2 else m_a
         m = jnp.where(lane_n < PAIRS, m_a, m_b)
-        if p < 2:
-            table = recv_l[:, BLOCK * p:BLOCK * p + BLOCK, :].astype(F32).reshape(HALF, 128)
-        else:
-            packed = recv_l[:, 2 * BLOCK:LEG_ROWS, :].astype(F32)
-            swapped = jnp.concatenate([packed[:, :, 64:128], packed[:, :, 0:64]], axis=2)
-            table = jnp.concatenate([packed[:, 0:40], swapped[:, 0:40]], axis=1).reshape(HALF, 128)
+        parts = []
+        for core in range(2):
+            if p < 2:
+                parts.append(recv_l[core, :, BLOCK * p:BLOCK * p + BLOCK, :].astype(F32))
+            else:
+                packed = recv_l[core, :, 2 * BLOCK:LEG_ROWS, :].astype(F32)
+                swapped = jnp.concatenate([packed[:, :, 64:128], packed[:, :, 0:64]], axis=2)
+                parts += [packed[:, 0:40], swapped[:, 0:40]]
+        table = jnp.concatenate(parts, axis=1).reshape(MW, 128)
         table = jnp.where(degree >= m, table, 0.0)
         rhs[p, :, 0:128] = table.astype(BF16)
         rhs[p, :, 128:256] = jnp.where(((degree + m) & 1) == 1, -table, table).astype(BF16)
 
-    row_r = lax.broadcasted_iota(jnp.int32, (512, 128), 0) & 31
+    row_r = lax.broadcasted_iota(jnp.int32, (256, 128), 0) & 31
     j_r = row_r - GROUP * jnp.floor((row_r.astype(F32) + 0.5) * 0.2).astype(jnp.int32)
     slot_j[...] = j_r
     lane_r = lax.broadcasted_iota(jnp.int32, (32, 128), 1)
     pltpu.make_async_copy(recv_s, recv_s, ss_recv).wait()
 
-    left = recv_s[...].reshape(512, HALF)
+    left = recv_s[...].reshape(256, MW)
     terms = [jnp.dot(left, rhs[p], preferred_element_type=F32) for p in range(3)]
     j_r = slot_j[...]
     north, south = [
@@ -299,22 +302,21 @@
     north = jnp.where(odd, pltpu.roll(north, PAIRS, 1), north)
     south = jnp.where(odd, south, pltpu.roll(south, PAIRS, 1))
     both_halves = jnp.where(lane_r[0:1, :] < PAIRS, north, south)
-    send_r[...] = both_halves.astype(BF16).reshape(LEVS, 32, 128)
+    send_r[...] = both_halves.astype(BF16).reshape(CHIPS, 32, 128)
 
     def level_copy(k):
-        to = lax.rem(me + k, LEVS)
+        to = lax.rem(z + k, CHIPS)
         return pltpu.make_async_remote_copy(
-            src_ref=send_r.at[to], dst_ref=recv_x.at[me], send_sem=sx_send,
-            recv_sem=sx_recv, device_id={"lev": to}, device_id_type=MESH,
+            src_ref=send_r.at[to], dst_ref=recv_x.at[z], send_sem=sx_send,
+            recv_sem=sx_recv, device_id={"lev": 2 * to + c}, device_id_type=MESH,
         )
 
-    for k in sorted(range(1, LEVS), key=lambda k: abs(k - LEVS // 2)):
+    for k in sorted(range(1, CHIPS), key=lambda k: abs(k - CHIPS // 2)):
         level_copy(k).start()
-    pltpu.make_async_copy(send_r.at[me], recv_x.at[me], sx_recv).start()
+    pltpu.make_async_copy(send_r.at[z], recv_x.at[z], sx_recv).start()
     pltpu.make_async_copy(recv_x, recv_x, sx_recv).wait()
 
-    got = recv_x[...].astype(F32).reshape(CHIPS, 2, 32, 128)
-    level_sums = (got[:, 0] + got[:, 1]).reshape(256, 128).astype(BF16)
+    level_sums = recv_x[...].reshape(256, 128)
     by_slot = nt_dot(onehot[...], level_sums)
     low = by_slot[:, 0:128].reshape(WAVES, 8, 128)
     high = by_slot[:, 128:256].reshape(WAVES, 8, 128)
@@ -374,17 +376,10 @@
         part = block.at[pl.ds(0, count)]
         pltpu.make_async_copy(part, part, sem).wait()
 
-    all_sent(recv_s, LEVS - 1, ss_send)
-
-    @pl.when(c == half)
-    def _():
-        all_sent(recv_l, CHIPS - 1, sl_send)
-
-    @pl.when(c != half)
-    def _():
-        all_sent(recv_l, CHIPS, sl_send)
-
-    all_sent(recv_x, LEVS - 1, sx_send)
+    all_sent(recv_s, CHIPS - 1, ss_send)
+    all_sent(recv_l.at[0], CHIPS - 1, sl_send)
+    all_sent(recv_l.at[0], CHIPS, sf_send)
+    all_sent(recv_x, CHIPS - 1, sx_send)
     all_sent(recv_z, WAVES - 1, sz_send)
 
 
@@ -408,14 +403,14 @@
             pltpu.VMEM((16, 128), jnp.int32),
             pltpu.VMEM((1, MW), F32),
             pltpu.VMEM((10, 256, 128), F32),
-            pltpu.VMEM((CHIPS, 2, 32, HALF), BF16),
+            pltpu.VMEM((CHIPS, 32, MW), BF16),
             pltpu.VMEM((CHIPS, LEG_ROWS, 128), BF16),
-            pltpu.VMEM((LEVS, 32, HALF), BF16),
-            pltpu.VMEM((8, LEG_ROWS, 128), BF16),
-            pltpu.VMEM((3, HALF, 256), BF16),
-            pltpu.VMEM((512, 128), jnp.int32),
-            pltpu.VMEM((LEVS, 32, 128), BF16),
-            pltpu.VMEM((LEVS, 32, 128), BF16),
+            pltpu.VMEM((CHIPS, 32, MW), BF16),
+            pltpu.VMEM((2, CHIPS, LEG_ROWS, 128), BF16),
+            pltpu.VMEM((3, MW, 256), BF16),
+            pltpu.VMEM((256, 128), jnp.int32),
+            pltpu.VMEM((CHIPS, 32, 128), BF16),
+            pltpu.VMEM((CHIPS, 32, 128), BF16),
             pltpu.VMEM((256, 128), BF16),
             pltpu.VMEM((WAVES, 16, 128), BF16),
             pltpu.VMEM((WAVES, 16, 128), BF16),
@@ -428,7 +423,7 @@
             pltpu.VMEM((LAT_MAX, 128, 2 * MW), BF16),
             pltpu.VMEM((LAT_MAX, 2 * MW, 128), BF16),
             pltpu.VMEM((1024, 128), F32),
-            dma((6,)), dma, dma, dma, dma, dma, dma, dma, dma,
+            dma((6,)), dma, dma, dma, dma((CHIPS,)), dma, dma, dma, dma, dma, dma,
         ],
         compiler_params=pltpu.CompilerParams(
             collective_id=0, has_side_effects=True, vmem_limit_bytes=58 * 2**20

time: 59.8 us -> 57.4 us (0.960)
  Pallas kernels: 58 us -> 55.5 us
    pallas_call x1, Pallas kernels: 58 us -> 55.5 us  [on_device(): pl.pallas_call(kernel, out_shape=jax.ShapeDtypeStruct((3, LAT_MAX, NLON_M...]
where the time goes in v4:
time: 57.4 us; the launch traced here: 57.2 us
  Pallas kernels  55.5 us (97%)
  local copies, waits for them, and re-layouts  1.66 us (3%)
    pallas_call x1, Pallas kernels, on_device(): pl.pallas_call(kernel, out_shape=jax.ShapeDtypeStruct((3, LAT_MAX, NLON_M...  55.5 us
    unnamed x1, local copies, waits for them, and re-layouts  1.66 us

profile of v4, /device:TPU:1, one launch (start us, length us, event | category | flops | bytes accessed | tf_op | source)
XLA Modules:
  0.0 57.2 jit_solution(16182561582703578710)
XLA Ops:
  0.0 55.5 %shard_map.55 = bf16[3,8,5136]{2,1,0:T(8,128)(2,1)} custom-call(s32[1280]{0:T(1024)} %mids_hbm.1, s32[32]{0:T(128)} %bands_hbm.1, s32[64]{0:T(128)} %nlon_hbm.1, bf16[240,1280]{1,0:T(8,128)(2,1)} %bitcast.10, bf16[40,64,80]{2,1,0:T(8,128)(2,1)} %bitcast.9, s32[10,128]{1,0:T(8,128)} %bitcast.11), custom_call_target="tpu_custom_call" | custom-call | tf_op jit(solution)/shard_map/pallas_call | solution.py:392
  55.5 1.7 %copy.8 = bf16[8,3,1,5136]{3,0,2,1:T(8,128)(2,1)} copy(bf16[8,3,1,5136]{3,0,2,1:T(8,128)(2,1)} %bitcast.8) | data formatting | bytes 493056

commit v5 on v4

--- a/solution.py
+++ b/solution.py
@@ -13,6 +13,7 @@
 CHIPS = 8
 SLOTS = 40
 GROUP = 5
+HALF = 640
 MW = 1280
 BLOCK = 80
 LEG_ROWS = 208
@@ -53,7 +54,7 @@
 def kernel(
     mids_hbm, bands_hbm, nlon_hbm, spec_hbm, leg_hbm, mids_rows_hbm, out_ref,
     mids_ref, bands_ref, nlon_ref, spec_ref, leg_ref, mids_rows, mrow_ref, spec_f, send_s, send_l, recv_s, recv_l, rhs, slot_j, send_r, recv_x,
-    onehot, send_y, recv_z, zf, zs, expand, mcol, cosc, sinc, tw, mod, lat,
+    onehot, send_y, recv_z, zf, zs, expand, mcol, cosc, sinc, tw, mod, partial, lat,
     load_sem, ss_send, ss_recv, sl_send, sl_recv, sf_send, sf_recv, sx_send, sx_recv, sz_send, sz_recv,
 ):
     w = lax.axis_index("wave")
@@ -100,6 +101,11 @@
     loads[0].wait()
     pl.semaphore_wait(barrier, CHIPS + WAVES - 1)
 
+    def first_chip(chip):
+        return (chip + 6 + (chip & 1)) & 7
+
+    own_first = first_chip(z)
+
     def spec_copy(k):
         to = lax.rem(z + k, CHIPS)
         return pltpu.make_async_remote_copy(
@@ -107,47 +113,55 @@
             recv_sem=ss_recv, device_id={"lev": 2 * to + c}, device_id_type=MESH,
         )
 
-    def leg_copy(k):
-        to = lax.rem(z + k, CHIPS)
+    def leg_copy(to):
+        seat = (z - first_chip(to)) & 7
         return pltpu.make_async_remote_copy(
-            src_ref=send_l.at[to], dst_ref=recv_l.at[c, z], send_sem=sl_send,
-            recv_sem=sl_recv.at[z], device_id={"lev": 2 * to + c}, device_id_type=MESH,
+            src_ref=send_l.at[to & 3], dst_ref=recv_l.at[c, seat], send_sem=sl_send,
+            recv_sem=sl_recv.at[seat], device_id={"lev": 2 * to + c}, device_id_type=MESH,
         )
 
-    def share_copy(chip):
+    def share_copy(seat):
         return pltpu.make_async_remote_copy(
-            src_ref=recv_l.at[c, chip], dst_ref=recv_l.at[c, chip], send_sem=sf_send,
+            src_ref=recv_l.at[c, seat], dst_ref=recv_l.at[c, seat], send_sem=sf_send,
             recv_sem=sf_recv, device_id={"lev": sibling}, device_id_type=MESH,
         )
 
     def order_of(i):
         return jnp.where(lax.rem(i, 2) == 1, 4 - (i + 1) // 2, 4 + i // 2)
 
-    def prepare_leg(k):
-        to = lax.rem(z + k, CHIPS)
+    def prepare_leg(low, gi):
+        group = low + 4 * gi
         for p in range(2):
-            stacked = jnp.concatenate([leg_ref[16 * p + to], leg_ref[16 * p + 8 + to]], axis=0)
-            send_l[to, BLOCK * p:BLOCK * p + BLOCK, :] = nt_dot(unit, stacked).astype(BF16)
-        last = leg_ref[32 + to].astype(F32)
+            stacked = jnp.concatenate([leg_ref[16 * p + group], leg_ref[16 * p + 8 + group]], axis=0)
+            send_l[low, gi, BLOCK * p:BLOCK * p + BLOCK, :] = nt_dot(unit, stacked).astype(BF16)
+        last = leg_ref[32 + group].astype(F32)
         stacked = jnp.where(upper, jnp.concatenate([last, last], axis=0), 0.0).astype(BF16)
-        send_l[to, 2 * BLOCK:LEG_ROWS, :] = nt_dot(fold, stacked).astype(BF16)
+        send_l[low, gi, 2 * BLOCK:LEG_ROWS, :] = nt_dot(fold, stacked).astype(BF16)
+
+    lane_s = lax.broadcasted_iota(jnp.int32, (32, 128), 1)
 
     def prepare_spec(k):
         to = lax.rem(z + k, CHIPS)
-        for tile in range(10):
-            rows = spec_f[tile, pl.ds(to, 32, stride=8), :].astype(BF16)
-            send_s[to, :, 128 * tile:128 * tile + 128] = rows
-
-    def send_leg(i, carry):
-        k = order_of(i)
-        prepare_leg(k)
-        leg_copy(k).start()
-        return carry
-
-    lax.fori_loop(0, CHIPS - 1, send_leg, 0)
-    prepare_leg(0)
-
-    pltpu.make_async_copy(send_l.at[z], recv_l.at[c, z], sl_recv.at[z]).start()
+        start = 2 * BLOCK * first_chip(to)
+        shift = start & 127
+        for gi in range(2):
+            turned = []
+            for u in range(6):
+                tile = lax.rem((start >> 7) + u, 10)
+                rows = spec_f[tile, pl.ds((to & 3) + 4 * gi, 32, stride=8), :]
+                turned.append(pltpu.roll(rows, (128 - shift) & 127, 1))
+            for u in range(5):
+                rows = jnp.where(lane_s < 128 - shift, turned[u], turned[u + 1])
+                send_s[to, 32 * gi:32 * gi + 32, 128 * u:128 * u + 128] = rows.astype(BF16)
+
+    for to in ((z + 2 - 4 * (z & 1)) & 7, (z + 1) & 7, (z + 7) & 7):
+        for gi in range(2):
+            prepare_leg(to & 3, gi)
+        leg_copy(to).start()
+    for gi in range(2):
+        prepare_leg(z & 3, gi)
+    own_seat = (z - own_first) & 7
+    pltpu.make_async_copy(send_l.at[z & 3], recv_l.at[c, own_seat], sl_recv.at[own_seat]).start()
 
     loads[1].wait()
     for tile in range(10):
@@ -207,9 +221,14 @@
     digits = jnp.concatenate([high, natural - 8.0 * high], axis=0).astype(BF16)
     for t in range(10):
         place = lax.broadcasted_iota(jnp.int32, (128, 128), 1) + 128 * t
-        group = place >> 6
+        wave_half = jnp.where(place >= HALF, 1, 0)
+        inner = place - HALF * wave_half
+        group = inner >> 5
         zl = jnp.where(group >= 5, 1, 0) + jnp.where(group >= 10, 1, 0) + jnp.where(group >= 15, 1, 0)
-        source = SLOTS * ((place & 63) >> 1) + 8 * (group - GROUP * zl) + 4 * (place & 1) + zl
+        seat = (inner & 31) >> 1
+        from_y = (w // 4 - (2 * (seat >> 2) + wave_half) + 8) & 7
+        from_x = ((w & 3) - (seat & 3) + 4) & 3
+        source = SLOTS * (4 * from_y + from_x) + 8 * (group - GROUP * zl) + 4 * (place & 1) + zl
         pick = lax.broadcasted_iota(jnp.int32, (128, 128), 0) == (source & 127)
         found = jnp.dot(digits, jnp.where(pick, 1.0, 0.0).astype(BF16), preferred_element_type=F32)
         found = 8.0 * found[0:16, :] + found[16:32, :]
@@ -238,8 +257,8 @@
         lax.fori_loop(0, 10, coarse, 0)
 
         def fine(i, inner_carry):
-            at = pl.multiple_of(128 * i, 128)
-            m = mrow_ref[0:1, pl.ds(at, 128)]
+            m = mrow_ref[0:1, pl.ds(pl.multiple_of(128 * i, 128), 128)]
+            at = pl.multiple_of(128 * i + jnp.where(i >= 5, HALF, 0), 128)
             weight = jnp.where(m == 0, 1.0, 2.0)
             weight = jnp.where(2 * m < cycle, weight, 0.0)
             cos_a, sin_a = cos_sin(m * a_steps, cycle, inverse)
@@ -249,7 +268,7 @@
             for a in range(8):
                 ca, sa = cos_a[a:a + 1, :], sin_a[a:a + 1, :]
                 tw[slot, 16 * a:16 * a + 16, pl.ds(at, 128)] = (ca * cos_b - sa * sin_b).astype(BF16)
-                other = pl.multiple_of(at + MW, 128)
+                other = pl.multiple_of(at + HALF, 128)
                 tw[slot, 16 * a:16 * a + 16, pl.ds(other, 128)] = (-(sa * cos_b + ca * sin_b)).astype(BF16)
             return inner_carry
 
@@ -258,32 +277,31 @@
 
     lax.fori_loop(0, LAT_MAX, tables, 0)
 
-    def share(i, carry):
-        chip = lax.rem(z - jnp.where(i == CHIPS - 1, 0, order_of(i)) + CHIPS, CHIPS)
-        pltpu.make_async_copy(recv_l.at[c, chip], recv_l.at[c, chip], sl_recv.at[chip]).wait()
-        share_copy(chip).start()
-        return carry
-
-    lax.fori_loop(0, CHIPS, share, 0)
+    for seat in range(4):
+        pltpu.make_async_copy(recv_l.at[c, seat], recv_l.at[c, seat], sl_recv.at[seat]).wait()
+        share_copy(seat).start()
     pltpu.make_async_copy(recv_l.at[1 - c], recv_l.at[1 - c], sf_recv).wait()
-    degree = lax.broadcasted_iota(jnp.int32, (MW, 128), 0)
-    lane_n = lax.broadcasted_iota(jnp.int32, (MW, 128), 1)
-    for p in range(3):
-        m_a = mids_ref[SLOTS * w + 16 * p + z]
-        m_b = mids_ref[SLOTS * w + 16 * p + 8 + z] if p < 2 else m_a
+    degree = lax.broadcasted_iota(jnp.int32, (HALF, 128), 0) + 2 * BLOCK * own_first
+    degree = jnp.where(degree >= MW, degree - MW, degree)
+    lane_n = lax.broadcasted_iota(jnp.int32, (HALF, 128), 1)
+    for gp in range(6):
+        gi, p = gp // 3, gp % 3
+        first_slot = SLOTS * w + 16 * p + (z & 3) + 4 * gi
+        m_a = mids_ref[first_slot]
+        m_b = mids_ref[first_slot + 8] if p < 2 else m_a
         m = jnp.where(lane_n < PAIRS, m_a, m_b)
         parts = []
         for core in range(2):
             if p < 2:
-                parts.append(recv_l[core, :, BLOCK * p:BLOCK * p + BLOCK, :].astype(F32))
+                parts.append(recv_l[core, :, gi, BLOCK * p:BLOCK * p + BLOCK, :].astype(F32))
             else:
-                packed = recv_l[core, :, 2 * BLOCK:LEG_ROWS, :].astype(F32)
+                packed = recv_l[core, :, gi, 2 * BLOCK:LEG_ROWS, :].astype(F32)
                 swapped = jnp.concatenate([packed[:, :, 64:128], packed[:, :, 0:64]], axis=2)
                 parts += [packed[:, 0:40], swapped[:, 0:40]]
-        table = jnp.concatenate(parts, axis=1).reshape(MW, 128)
+        table = jnp.concatenate(parts, axis=1).reshape(HALF, 128)
         table = jnp.where(degree >= m, table, 0.0)
-        rhs[p, :, 0:128] = table.astype(BF16)
-        rhs[p, :, 128:256] = jnp.where(((degree + m) & 1) == 1, -table, table).astype(BF16)
+        rhs[gp, :, 0:128] = table.astype(BF16)
+        rhs[gp, :, 128:256] = jnp.where(((degree + m) & 1) == 1, -table, table).astype(BF16)
 
     row_r = lax.broadcasted_iota(jnp.int32, (256, 128), 0) & 31
     j_r = row_r - GROUP * jnp.floor((row_r.astype(F32) + 0.5) * 0.2).astype(jnp.int32)
@@ -291,18 +309,19 @@
     lane_r = lax.broadcasted_iota(jnp.int32, (32, 128), 1)
     pltpu.make_async_copy(recv_s, recv_s, ss_recv).wait()
 
-    left = recv_s[...].reshape(256, MW)
-    terms = [jnp.dot(left, rhs[p], preferred_element_type=F32) for p in range(3)]
-    j_r = slot_j[...]
-    north, south = [
-        jnp.where(j_r >= 4, terms[2][:, at:at + 128], jnp.where(j_r >= 2, terms[1][:, at:at + 128], terms[0][:, at:at + 128]))
-        for at in (0, 128)
-    ]
-    odd = (j_r & 1) == 1
-    north = jnp.where(odd, pltpu.roll(north, PAIRS, 1), north)
-    south = jnp.where(odd, south, pltpu.roll(south, PAIRS, 1))
-    both_halves = jnp.where(lane_r[0:1, :] < PAIRS, north, south)
-    send_r[...] = both_halves.astype(BF16).reshape(CHIPS, 32, 128)
+    for gi in range(2):
+        left = recv_s[:, 32 * gi:32 * gi + 32, :].reshape(256, HALF)
+        terms = [jnp.dot(left, rhs[3 * gi + p], preferred_element_type=F32) for p in range(3)]
+        j_r = slot_j[...]
+        north, south = [
+            jnp.where(j_r >= 4, terms[2][:, at:at + 128], jnp.where(j_r >= 2, terms[1][:, at:at + 128], terms[0][:, at:at + 128]))
+            for at in (0, 128)
+        ]
+        odd = (j_r & 1) == 1
+        north = jnp.where(odd, pltpu.roll(north, PAIRS, 1), north)
+        south = jnp.where(odd, south, pltpu.roll(south, PAIRS, 1))
+        both_halves = jnp.where(lane_r[0:1, :] < PAIRS, north, south)
+        send_r[:, 32 * gi:32 * gi + 32, :] = both_halves.astype(BF16).reshape(CHIPS, 32, 128)
 
     def level_copy(k):
         to = lax.rem(z + k, CHIPS)
@@ -316,49 +335,53 @@
     pltpu.make_async_copy(send_r.at[z], recv_x.at[z], sx_recv).start()
     pltpu.make_async_copy(recv_x, recv_x, sx_recv).wait()
 
-    level_sums = recv_x[...].reshape(256, 128)
+    got = recv_x[...].astype(F32)
+    got = got[0:4] + got[4:8]
+    level_sums = jnp.concatenate([got[:, 0:32], got[:, 32:64]], axis=0).reshape(256, 128).astype(BF16)
     by_slot = nt_dot(onehot[...], level_sums)
     low = by_slot[:, 0:128].reshape(WAVES, 8, 128)
     high = by_slot[:, 128:256].reshape(WAVES, 8, 128)
     send_y[...] = jnp.concatenate([low, high], axis=1).astype(BF16)
 
-    def band_copy(k):
-        to = lax.rem(w + k, WAVES)
+    def band_copy(dy, dx):
+        to = 4 * ((w // 4 + dy) & 7) + ((w + dx) & 3)
+        seat = 16 * (dy % 2) + 4 * (dy // 2) + dx
         return pltpu.make_async_remote_copy(
-            src_ref=send_y.at[to], dst_ref=recv_z.at[w], send_sem=sz_send,
-            recv_sem=sz_recv, device_id={"wave": to}, device_id_type=MESH,
+            src_ref=send_y.at[to], dst_ref=recv_z.at[seat], send_sem=sz_send,
+            recv_sem=sz_recv.at[dy % 2], device_id={"wave": to}, device_id_type=MESH,
         )
 
-    for k in sorted(range(1, WAVES), key=lambda k: abs(k - WAVES // 2)):
-        band_copy(k).start()
-    pltpu.make_async_copy(send_y.at[w], recv_z.at[w], sz_recv).start()
-    pltpu.make_async_copy(recv_z, recv_z, sz_recv).wait()
-
-    zf[...] = recv_z[...].astype(F32).reshape(512, 128)
-    for slot in range(LAT_MAX):
-        zs[64 * slot:64 * slot + 64, :] = zf[pl.ds(slot, 64, stride=8), :].astype(BF16)
-
-    def modulate(i, carry):
-        both = jnp.dot(zs[...], expand[i], preferred_element_type=F32)
-        at = pl.multiple_of(64 * i, 64)
-        other = pl.multiple_of(64 * i + MW, 64)
+    moves = [(dy, dx) for dy in (4, 2, 6, 0, 3, 5, 1, 7) for dx in (2, 1, 3, 0) if dy or dx]
+    for dy, dx in moves:
+        band_copy(dy, dx).start()
+    pltpu.make_async_copy(send_y.at[w], recv_z.at[0], sz_recv.at[0]).start()
+
+    for part in range(2):
+        arrived = recv_z.at[pl.ds(16 * part, 16)]
+        pltpu.make_async_copy(arrived, arrived, sz_recv.at[part]).wait()
+        zf[...] = arrived[...].astype(F32).reshape(256, 128)
         for slot in range(LAT_MAX):
-            re = both[64 * slot:64 * slot + 64, 0:128]
-            im = both[64 * slot:64 * slot + 64, 128:256]
-            cos_part = cosc[slot, pl.ds(at, 64), :]
-            sin_part = sinc[slot, pl.ds(at, 64), :]
-            mod[slot, pl.ds(at, 64), :] = (re * cos_part - im * sin_part).astype(BF16)
-            mod[slot, pl.ds(other, 64), :] = (re * sin_part + im * cos_part).astype(BF16)
-        return carry
-
-    lax.fori_loop(0, 20, modulate, 0, unroll=20)
-
-    def transform(slot, carry):
-        points = jnp.dot(tw[slot], mod[slot], preferred_element_type=F32)
-        lat[pl.ds(slot, 128, stride=8), :] = points.T
-        return carry
-
-    lax.fori_loop(0, LAT_MAX, transform, 0, unroll=8)
+            zs[32 * slot:32 * slot + 32, :] = zf[pl.ds(slot, 32, stride=8), :].astype(BF16)
+        for i in range(20):
+            both = jnp.dot(zs[...], expand[i], preferred_element_type=F32)
+            table_at = HALF * part + 32 * i
+            at = MW * part + 32 * i
+            for slot in range(LAT_MAX):
+                re = both[32 * slot:32 * slot + 32, 0:128]
+                im = both[32 * slot:32 * slot + 32, 128:256]
+                cos_part = cosc[slot, table_at:table_at + 32, :]
+                sin_part = sinc[slot, table_at:table_at + 32, :]
+                mod[slot, at:at + 32, :] = (re * cos_part - im * sin_part).astype(BF16)
+                mod[slot, at + HALF:at + HALF + 32, :] = (re * sin_part + im * cos_part).astype(BF16)
+        for slot in range(LAT_MAX):
+            points = jnp.dot(
+                tw[slot, :, MW * part:MW * part + MW], mod[slot, MW * part:MW * part + MW, :],
+                preferred_element_type=F32,
+            )
+            if part == 0:
+                partial[slot] = points
+            else:
+                lat[pl.ds(slot, 128, stride=8), :] = (partial[slot] + points).T
 
     slot_of = lax.broadcasted_iota(jnp.int32, (8, 128), 0)
     lon = lax.broadcasted_iota(jnp.int32, (8, 128), 1)
@@ -377,10 +400,10 @@
         pltpu.make_async_copy(part, part, sem).wait()
 
     all_sent(recv_s, CHIPS - 1, ss_send)
-    all_sent(recv_l.at[0], CHIPS - 1, sl_send)
-    all_sent(recv_l.at[0], CHIPS, sf_send)
+    all_sent(recv_l.at[0], 3, sl_send)
+    all_sent(recv_l.at[0], 4, sf_send)
     all_sent(recv_x, CHIPS - 1, sx_send)
-    all_sent(recv_z, WAVES - 1, sz_send)
+    all_sent(send_y, WAVES - 1, sz_send)
 
 
 def on_device(spec, legendre, mids, band_lats, nlon):
@@ -403,27 +426,28 @@
             pltpu.VMEM((16, 128), jnp.int32),
             pltpu.VMEM((1, MW), F32),
             pltpu.VMEM((10, 256, 128), F32),
-            pltpu.VMEM((CHIPS, 32, MW), BF16),
-            pltpu.VMEM((CHIPS, LEG_ROWS, 128), BF16),
-            pltpu.VMEM((CHIPS, 32, MW), BF16),
-            pltpu.VMEM((2, CHIPS, LEG_ROWS, 128), BF16),
-            pltpu.VMEM((3, MW, 256), BF16),
+            pltpu.VMEM((CHIPS, 64, HALF), BF16),
+            pltpu.VMEM((4, 2, LEG_ROWS, 128), BF16),
+            pltpu.VMEM((CHIPS, 64, HALF), BF16),
+            pltpu.VMEM((2, 4, 2, LEG_ROWS, 128), BF16),
+            pltpu.VMEM((6, HALF, 256), BF16),
             pltpu.VMEM((256, 128), jnp.int32),
-            pltpu.VMEM((CHIPS, 32, 128), BF16),
-            pltpu.VMEM((CHIPS, 32, 128), BF16),
+            pltpu.VMEM((CHIPS, 64, 128), BF16),
+            pltpu.VMEM((CHIPS, 64, 128), BF16),
             pltpu.VMEM((256, 128), BF16),
             pltpu.VMEM((WAVES, 16, 128), BF16),
             pltpu.VMEM((WAVES, 16, 128), BF16),
-            pltpu.VMEM((512, 128), F32),
-            pltpu.VMEM((512, 128), BF16),
+            pltpu.VMEM((256, 128), F32),
+            pltpu.VMEM((256, 128), BF16),
             pltpu.VMEM((20, 128, 256), BF16),
             pltpu.VMEM((MW, 128), F32),
             pltpu.VMEM((LAT_MAX, MW, 128), F32),
             pltpu.VMEM((LAT_MAX, MW, 128), F32),
             pltpu.VMEM((LAT_MAX, 128, 2 * MW), BF16),
             pltpu.VMEM((LAT_MAX, 2 * MW, 128), BF16),
+            pltpu.VMEM((LAT_MAX, 128, 128), F32),
             pltpu.VMEM((1024, 128), F32),
-            dma((6,)), dma, dma, dma, dma((CHIPS,)), dma, dma, dma, dma, dma, dma,
+            dma((6,)), dma, dma, dma, dma((4,)), dma, dma, dma, dma, dma, dma((2,)),
         ],
         compiler_params=pltpu.CompilerParams(
             collective_id=0, has_side_effects=True, vmem_limit_bytes=58 * 2**20

time: 57.4 us -> 53.7 us (0.936)
  Pallas kernels: 55.5 us -> 51.9 us
    pallas_call x1, Pallas kernels: 55.5 us -> 51.9 us  [on_device(): pl.pallas_call(kernel, out_shape=jax.ShapeDtypeStruct((3, LAT_MAX, NLON_M...]
where the time goes in v5:
time: 53.7 us; the launch traced here: 53.6 us
  Pallas kernels  51.9 us (97%)
  local copies, waits for them, and re-layouts  1.66 us (3%)
    pallas_call x1, Pallas kernels, on_device(): pl.pallas_call(kernel, out_shape=jax.ShapeDtypeStruct((3, LAT_MAX, NLON_M...  51.9 us
    unnamed x1, local copies, waits for them, and re-layouts  1.66 us

profile of v5, /device:TPU:1, one launch (start us, length us, event | category | flops | bytes accessed | tf_op | source)
XLA Modules:
  0.0 53.6 jit_solution(16459030397565790988)
XLA Ops:
  0.0 51.9 %shard_map.55 = bf16[3,8,5136]{2,1,0:T(8,128)(2,1)} custom-call(s32[1280]{0:T(1024)} %mids_hbm.1, s32[32]{0:T(128)} %bands_hbm.1, s32[64]{0:T(128)} %nlon_hbm.1, bf16[240,1280]{1,0:T(8,128)(2,1)} %bitcast.10, bf16[40,64,80]{2,1,0:T(8,128)(2,1)} %bitcast.9, s32[10,128]{1,0:T(8,128)} %bitcast.11), custom_call_target="tpu_custom_call" | custom-call | tf_op jit(solution)/shard_map/pallas_call | solution.py:415
  51.9 1.7 %copy.8 = bf16[8,3,1,5136]{3,0,2,1:T(8,128)(2,1)} copy(bf16[8,3,1,5136]{3,0,2,1:T(8,128)(2,1)} %bitcast.8) | data formatting | bytes 493056

commit v6 on v5

--- a/solution.py
+++ b/solution.py
@@ -99,7 +99,6 @@
         lax.broadcasted_iota(jnp.int32, (LATS, BLOCK), 1) < 40
     )
     loads[0].wait()
-    pl.semaphore_wait(barrier, CHIPS + WAVES - 1)
 
     def first_chip(chip):
         return (chip + 6 + (chip & 1)) & 7
@@ -154,28 +153,30 @@
                 rows = jnp.where(lane_s < 128 - shift, turned[u], turned[u + 1])
                 send_s[to, 32 * gi:32 * gi + 32, 128 * u:128 * u + 128] = rows.astype(BF16)
 
-    for to in ((z + 2 - 4 * (z & 1)) & 7, (z + 1) & 7, (z + 7) & 7):
+    for low in range(4):
         for gi in range(2):
-            prepare_leg(to & 3, gi)
-        leg_copy(to).start()
-    for gi in range(2):
-        prepare_leg(z & 3, gi)
-    own_seat = (z - own_first) & 7
-    pltpu.make_async_copy(send_l.at[z & 3], recv_l.at[c, own_seat], sl_recv.at[own_seat]).start()
-
+            prepare_leg(low, gi)
     loads[1].wait()
     for tile in range(10):
         spec_f[tile, 0:240, :] = spec_ref[:, 128 * tile:128 * tile + 128].astype(F32)
         spec_f[tile, 240:256, :] = jnp.zeros((16, 128), F32)
 
+    def prepare_all(k, carry):
+        prepare_spec(k)
+        return carry
+
+    lax.fori_loop(0, CHIPS, prepare_all, 0)
+    pl.semaphore_wait(barrier, CHIPS + WAVES - 1)
+    for to in ((z + 2 - 4 * (z & 1)) & 7, (z + 1) & 7, (z + 7) & 7):
+        leg_copy(to).start()
+    own_seat = (z - own_first) & 7
+    pltpu.make_async_copy(send_l.at[z & 3], recv_l.at[c, own_seat], sl_recv.at[own_seat]).start()
+
     def send_spec(i, carry):
-        k = order_of(i)
-        prepare_spec(k)
-        spec_copy(k).start()
+        spec_copy(order_of(i)).start()
         return carry
 
-    lax.fori_loop(0, CHIPS - 1, send_spec, 0)
-    prepare_spec(0)
+    lax.fori_loop(0, CHIPS - 1, send_spec, 0, unroll=7)
     pltpu.make_async_copy(send_s.at[z], recv_s.at[z], ss_recv).start()
 
     for load in loads[2:]:

time: 53.7 us -> 52.9 us (0.985)
  Pallas kernels: 51.9 us -> 51.1 us
    pallas_call x1, Pallas kernels: 51.9 us -> 51.1 us  [on_device(): pl.pallas_call(kernel, out_shape=jax.ShapeDtypeStruct((3, LAT_MAX, NLON_M...]
where the time goes in v6:
time: 52.9 us; the launch traced here: 52.8 us
  Pallas kernels  51.1 us (97%)
  local copies, waits for them, and re-layouts  1.66 us (3%)
    pallas_call x1, Pallas kernels, on_device(): pl.pallas_call(kernel, out_shape=jax.ShapeDtypeStruct((3, LAT_MAX, NLON_M...  51.1 us
    unnamed x1, local copies, waits for them, and re-layouts  1.66 us

profile of v6, /device:TPU:1, one launch (start us, length us, event | category | flops | bytes accessed | tf_op | source)
XLA Modules:
  0.0 52.8 jit_solution(15007051293599620499)
XLA Ops:
  0.0 51.1 %shard_map.55 = bf16[3,8,5136]{2,1,0:T(8,128)(2,1)} custom-call(s32[1280]{0:T(1024)} %mids_hbm.1, s32[32]{0:T(128)} %bands_hbm.1, s32[64]{0:T(128)} %nlon_hbm.1, bf16[240,1280]{1,0:T(8,128)(2,1)} %bitcast.10, bf16[40,64,80]{2,1,0:T(8,128)(2,1)} %bitcast.9, s32[10,128]{1,0:T(8,128)} %bitcast.11), custom_call_target="tpu_custom_call" | custom-call | tf_op jit(solution)/shard_map/pallas_call | solution.py:416
  51.1 1.7 %copy.8 = bf16[8,3,1,5136]{3,0,2,1:T(8,128)(2,1)} copy(bf16[8,3,1,5136]{3,0,2,1:T(8,128)(2,1)} %bitcast.8) | data formatting | bytes 493056

commit v7 on v6

--- a/solution.py
+++ b/solution.py
@@ -352,12 +352,12 @@
             recv_sem=sz_recv.at[dy % 2], device_id={"wave": to}, device_id_type=MESH,
         )
 
-    moves = [(dy, dx) for dy in (4, 2, 6, 0, 3, 5, 1, 7) for dx in (2, 1, 3, 0) if dy or dx]
+    moves = [(dy, dx) for dy in (3, 5, 1, 7, 4, 2, 6, 0) for dx in (2, 1, 3, 0) if dy or dx]
     for dy, dx in moves:
         band_copy(dy, dx).start()
     pltpu.make_async_copy(send_y.at[w], recv_z.at[0], sz_recv.at[0]).start()
 
-    for part in range(2):
+    for part in (1, 0):
         arrived = recv_z.at[pl.ds(16 * part, 16)]
         pltpu.make_async_copy(arrived, arrived, sz_recv.at[part]).wait()
         zf[...] = arrived[...].astype(F32).reshape(256, 128)
@@ -379,7 +379,7 @@
                 tw[slot, :, MW * part:MW * part + MW], mod[slot, MW * part:MW * part + MW, :],
                 preferred_element_type=F32,
             )
-            if part == 0:
+            if part == 1:
                 partial[slot] = points
             else:
                 lat[pl.ds(slot, 128, stride=8), :] = (partial[slot] + points).T
@@ -451,7 +451,7 @@
             dma((6,)), dma, dma, dma, dma((4,)), dma, dma, dma, dma, dma, dma((2,)),
         ],
         compiler_params=pltpu.CompilerParams(
-            collective_id=0, has_side_effects=True, vmem_limit_bytes=58 * 2**20
+            collective_id=0, has_side_effects=True, vmem_limit_bytes=56098816
         ),
     )(mids, band_lats, nlon, spec_rows, tables, mids.reshape(10, 128))
     return jnp.transpose(planes, (1, 0, 2)).reshape(LAT_MAX, 3, 1, NLON_MAX)

time: 52.9 us -> 52.6 us (level); the launches traced: 52.8 us -> 51.8 us
  Pallas kernels: 51.1 us -> 49.7 us
    pallas_call x1, Pallas kernels: 51.1 us -> 49.7 us  [on_device(): pl.pallas_call(kernel, out_shape=jax.ShapeDtypeStruct((3, LAT_MAX, NLON_M...]
    unnamed x1 -> x7, local copies, waits for them, and re-layouts: 1.66 us -> 2.06 us
where the time goes in v7:
time: 52.6 us; the launch traced here: 51.8 us
  Pallas kernels  49.7 us (94%)
  local copies, waits for them, and re-layouts  2.06 us (4%)
    pallas_call x1, Pallas kernels, on_device(): pl.pallas_call(kernel, out_shape=jax.ShapeDtypeStruct((3, LAT_MAX, NLON_M...  49.7 us
    unnamed x7, local copies, waits for them, and re-layouts  2.06 us

profile of v7, /device:TPU:1, one launch (start us, length us, event | category | flops | bytes accessed | tf_op | source)
XLA Modules:
  0.0 51.8 jit_solution(18180578178079460369)
XLA Ops:
  0.0 0.0 copy-start.1
  0.0 0.0 copy-start.2
  0.0 0.7 %copy-done.1 = s32[32]{0:T(128)S(1)} copy-done((s32[32]{0:T(128)S(1)}, s32[32]{0:T(128)}, u32[]{:S(2)}) %copy-start.1) | copy-done | bytes 152
  0.7 0.0 copy-done.2
  0.7 0.0 copy-start
  0.7 0.7 %copy-done = s32[1280]{0:T(1024)S(1)} copy-done((s32[1280]{0:T(1024)S(1)}, s32[1280]{0:T(1024)}, u32[]{:S(2)}) %copy-start) | copy-done | bytes 5144
  1.4 49.7 %shard_map.55 = bf16[3,8,5136]{2,1,0:T(8,128)(2,1)S(1)} custom-call(s32[1280]{0:T(1024)S(1)} %copy-done, s32[32]{0:T(128)S(1)} %copy-done.1, s32[64]{0:T(128)S(1)} %copy-done.2, bf16[240,1280]{1,0:T(8,128)(2,1)} %bitcast.11, bf16[40,64,80]{2,1,0:T(8,128)(2,1)} %bitcast.10, s32[10,128]{1,0:T(8,128)S(1)} %bitcast.9), custom_call_target="tpu_custom_call" | custom-call | tf_op jit(solution)/shard_map/pallas_call | solution.py:416
  51.1 0.7 %copy.8 = bf16[8,3,1,5136]{3,0,2,1:T(8,128)(2,1)} copy(bf16[8,3,1,5136]{3,0,2,1:T(8,128)(2,1)S(1)} %bitcast.8) | data formatting | bytes 493056
Async XLA Ops:
  0.0 0.7 %copy-start.1 = (s32[32]{0:T(128)S(1)}, s32[32]{0:T(128)}, u32[]{:S(2)}) copy-start(s32[32]{0:T(128)} %bands_hbm.1) | copy-start | bytes 388
  0.0 0.7 %copy-start.2 = (s32[64]{0:T(128)S(1)}, s32[64]{0:T(128)}, u32[]{:S(2)}) copy-start(s32[64]{0:T(128)} %nlon_hbm.1) | copy-start | bytes 772
  0.7 0.7 %copy-start = (s32[1280]{0:T(1024)S(1)}, s32[1280]{0:T(1024)}, u32[]{:S(2)}) copy-start(s32[1280]{0:T(1024)} %mids_hbm.1) | copy-start | bytes 15364
